TPU v7x, 32 devices: a whole 2x2x4 slice. The times are simulated.
32 devices in a mesh: groups: 2 (over y), sector: 16 (over z, x, core).
Axes of the slice: x: 2, y: 2, z: 4, core: 2. Of those that a mesh axis runs over, the one named last changes fastest.
Arguments:
- wavefunction: bfloat16 [32768, 128], P(('groups', 'sector')), parts along dimension 0, may hold values from -90 to 90
- env_left: bfloat16 [256, 40, 128, 128], P(('groups', 'sector')), parts along dimension 0, may hold values from -3 to 3
- right_environment_terms: bfloat16 [80, 128, 128], P('groups'), parts along dimension 0, may hold values from -1 to 1
- source_tile_lookup: int32 [256, 10], P('groups'), parts along dimension 0, may hold values from 0 to 127, as said below
Outputs:
- image_three: float32 [32768, 128], P(('groups', 'sector')), parts along dimension 0
- projected: float32 [6, 3], P('groups'), parts along dimension 0
There are 2 independent parts, one for each index of `groups`. A program takes and returns all parts, laid end to end along the dimension named above; each array names one. Nothing has to cross between parts.
Inputs may be any that keep to these rules, and one draw needn't show every extreme that they name: `source_tile_lookup`: entry 0 of output tile i is i itself. Of the other 8 x (9) entries of one device's output tiles, none names a tile of that device, at most 10 name tiles held by any one other device, and exactly 10 for some device.
All inputs are finite; a program needn't handle non-finite values.
Results may differ from a plain program's by a relative error of at most 0.0076.
Values may be sent and summed in bfloat16 or wider, within the bound.
No kernel may reach another device: no remote copies, remote signals or barrier semaphores. Data moves between devices by JAX's collectives and lax.ppermute only.
A program may use at most 128 MiB of HBM per device.

v0:
```python
import functools

import jax
import jax.numpy as jnp
from jax import lax
from jax.experimental import pallas as pl
from jax.experimental.pallas import tpu as pltpu
from jax.sharding import PartitionSpec as P

epsilon = 1e-06
f32 = jnp.float32
bf16 = jnp.bfloat16
STAT_ROWS = 16
LOADS = 4


def row(value):
    return jnp.broadcast_to(value, (1, 128))


def lane_sums(product):
    return jnp.sum(product, axis=0, keepdims=True)


def split_rows(sums):
    rows = []
    for value in sums:
        high = value.astype(bf16)
        rest = value - high.astype(f32)
        middle = rest.astype(bf16)
        low = (rest - middle.astype(f32)).astype(bf16)
        rows += [high, middle, low]
    rows += [jnp.zeros((1, 128), bf16)] * (STAT_ROWS - len(rows))
    return jnp.concatenate([r.astype(f32) for r in rows], axis=0).astype(bf16)


def start_kernel(w_ref, piece_ref):
    rows = w_ref.shape[0]
    w = w_ref[...]
    piece_ref[0:rows, :] = w
    wide = w.astype(f32)
    piece_ref[rows:, :] = split_rows([lane_sums(wide * wide)])


def ring_place(chip, chips):
    return jnp.where(chip % 2 == 0, chip // 2, chips - 1 - chip // 2)


def prepare_kernel(sizes, phases, peers, ring, own_ref, first_ref, second_ref, env_ref, *rest):
    count_ref, list_ref, stat_ref, env_out, first, second, sems = rest
    tile_dev, shifts, group, tile_rows, total = sizes
    records = tile_dev * shifts
    large = pltpu.make_async_copy(env_ref, env_out, sems.at[0])
    large.start()
    small = [
        pltpu.make_async_copy(first_ref, first, sems.at[1]),
        pltpu.make_async_copy(second_ref, second, sems.at[2]),
    ]
    for copy in small:
        copy.start()
    for p in range(phases):
        count_ref[p] = 0

    if ring:
        own = own_ref[0]
        core = own % 2
        chips = peers // 2
        here = ring_place(own // 2, chips)
        for d in range(peers):
            ahead = here - (d // 4 if d // 2 % 2 == 0 else chips - 1 - d // 4)
            ahead = jnp.where(ahead < 0, ahead + chips, ahead)
            steps = jnp.where(core == 0, ahead, jnp.where(ahead == 0, 0, chips - ahead))
            other = core if d % 2 == 0 else 1 - core
            slot = jnp.where(
                steps < chips // 2, 4 * steps - 2 + 2 * other, 4 * (chips - steps) + 1 - 2 * other
            )
            slot = jnp.where(steps == chips // 2, 2 * chips - 2 + other, slot)
            stat_ref[d] = jnp.where(steps == 0, other, slot) * STAT_ROWS
    else:

        def one_place(d, carry):
            stat_ref[d] = d * STAT_ROWS
            return carry

        lax.fori_loop(0, peers, one_place, 0)
    for copy in small:
        copy.wait()

    def one_tile(tile, carry):
        for shift in range(shifts):
            r = tile * shifts + shift
            if ring:
                source = first[r]
                device = lax.div(source, tile_dev)
                p = lax.div(stat_ref[device], STAT_ROWS)
                offset = (source - device * tile_dev) * tile_rows
            else:
                p, offset = first[r], second[r]
            n = count_ref[p]
            list_ref[0, p * records + n] = offset
            list_ref[1, p * records + n] = r * group * tile_rows
            list_ref[2, p * records + n] = (shift * tile_dev + tile) * tile_rows
            count_ref[p] = n + 1
        return carry

    lax.fori_loop(0, tile_dev, one_tile, 0)
    large.wait()


def contract_left(phase, unroll, sizes, count_ref, list_ref, buf_ref, env_ref, left_ref):
    tile_dev, shifts, group, tile_rows, total = sizes
    base = phase * tile_dev * shifts
    width = group * tile_rows
    count = count_ref[phase]

    def one(n):
        offset = pl.multiple_of(list_ref[0, n], 16)
        start = pl.multiple_of(list_ref[1, n], 128)
        target = pl.multiple_of(list_ref[2, n], 128)
        picked = buf_ref[pl.ds(offset, tile_rows), :]
        for t in range(group):
            left_ref[pl.ds(target, tile_rows), t * 128 : (t + 1) * 128] = jnp.dot(
                env_ref[pl.ds(start + t * tile_rows, tile_rows), :],
                picked,
                preferred_element_type=f32,
            ).astype(bf16)

    def some(j, carry):
        for q in range(unroll):
            one(base + jnp.minimum(j * unroll + q, count - 1))
        return carry

    lax.fori_loop(0, (count + unroll - 1) // unroll, some, 0)


def left_kernel(phase, unroll, sizes, count_ref, list_ref, buf_ref, env_ref, *rest):
    contract_left(phase, unroll, sizes, count_ref, list_ref, buf_ref, env_ref, rest[-1])


def apply_kernel(stage, sizes, slots, stat_ref, right_ref, w_ref, *rest):
    tile_dev, shifts, group, tile_rows, total = sizes
    rows = tile_dev * tile_rows
    phases = max(p for p, _ in slots) + 1
    bufs, rest = rest[:phases], rest[phases:]
    prior, rest = rest[: stage - 1], rest[stage - 1 :]
    if stage > 1:
        coef_in, rest = rest[0], rest[1:]
    left_ref, image_ref, coef_ref, send_ref, all_stats = rest

    width = group * tile_rows
    applied = jnp.zeros((rows, 128), f32)
    for k in range(shifts):
        applied = applied + jnp.dot(
            left_ref[k * rows : (k + 1) * rows, :],
            right_ref[k * width : (k + 1) * width, :],
            preferred_element_type=f32,
        )

    for n, (p, offset) in enumerate(slots):
        all_stats[n * STAT_ROWS : (n + 1) * STAT_ROWS, :] = bufs[p][offset : offset + STAT_ROWS, :]
    gathered = jnp.zeros((STAT_ROWS, 128), f32)
    for d in range(stat_ref.shape[0]):
        offset = pl.multiple_of(stat_ref[d], 16)
        gathered = gathered + all_stats[pl.ds(offset, STAT_ROWS), :].astype(f32)

    def mean_of(j):
        lanes = gathered[3 * j : 3 * j + 1] + gathered[3 * j + 1 : 3 * j + 2]
        lanes = lanes + gathered[3 * j + 2 : 3 * j + 3]
        return row(jnp.sum(lanes, axis=1, keepdims=True) * (1.0 / total))

    w = w_ref[...].astype(f32)
    if stage == 1:
        square = mean_of(0)
        scale = lax.rsqrt(square + epsilon)
        coefs = [scale, scale * scale * square]
        image = scale * applied
        sums = [lane_sums((w * scale) * image), lane_sums(image * image)]
    elif stage == 2:
        scale, g11 = coef_in[0:1, :], coef_in[1:2, :]
        aa, norm = mean_of(0), mean_of(1)
        rest_square = jnp.maximum(norm - 2.0 * aa * aa + aa * aa * g11, 0.0)
        ba = jnp.sqrt(rest_square + epsilon)
        g12 = (aa - aa * g11) / ba
        g22 = rest_square / (ba * ba)
        coefs = [scale, g11, aa, ba, g12, g22]
        first = prior[0][...]
        basis_one = w * scale
        basis_two = (first - aa * basis_one) / ba
        image = (applied - aa * first) / ba
        sums = [
            lane_sums(basis_one * image),
            lane_sums(basis_two * image),
            lane_sums(image * image),
        ]
    else:
        scale, g11, aa, ba, g12, g22 = [coef_in[j : j + 1, :] for j in range(6)]
        ab, bb, norm = mean_of(0), mean_of(1), mean_of(2)
        rest_square = norm - 2.0 * (ab * ab + bb * bb) + ab * ab * g11 + bb * bb * g22
        rest_square = jnp.maximum(rest_square + 2.0 * ab * bb * g12, 0.0)
        cb = jnp.sqrt(rest_square + epsilon)
        coefs = [aa, ab, ba, bb, cb]
        first, second = prior[0][...], prior[1][...]
        basis_one = w * scale
        basis_two = (first - aa * basis_one) / ba
        basis_three = (second - ab * basis_one - bb * basis_two) / cb
        image = (applied - ab * first - bb * second) / cb
        sums = [lane_sums(b * image) for b in (basis_one, basis_two, basis_three)]

    image_ref[...] = image
    coef_ref[...] = jnp.concatenate(coefs + [jnp.zeros((1, 128), f32)] * (8 - len(coefs)), axis=0)
    if stage < 3:
        rows = image.shape[0]
        send_ref[0:rows, :] = image.astype(bf16)
        send_ref[rows:, :] = split_rows(sums)
    else:
        send_ref[...] = jnp.concatenate(sums + [jnp.zeros((1, 128), f32)] * 5, axis=0)


def finish_kernel(total, stat_ref, coef_ref, out_ref):
    last = [row(jnp.sum(stat_ref[j : j + 1, :], axis=1, keepdims=True) * (1.0 / total)) for j in range(3)]
    aa, ab, ba, bb, cb = [coef_ref[j : j + 1, :] for j in range(5)]
    lane = lax.broadcasted_iota(jnp.int32, (1, 128), 1)

    def line(a, b, c):
        return jnp.where(lane == 0, a, jnp.where(lane == 1, b, c))

    zero = jnp.zeros((1, 128), f32)
    table = jnp.concatenate(
        [line(aa, ab, last[0]), line(ba, bb, last[1]), line(zero, cb, last[2])], axis=0
    )
    out_ref[...] = table[:, 0:3]


def ring_pairs(peers):
    chips = peers // 2
    order = list(range(0, chips, 2)) + list(range(chips - 1, 0, -2))
    pairs = []
    for j in range(chips):
        here, after = order[j] * 2, order[(j + 1) % chips] * 2
        pairs += [(here, after), (after + 1, here + 1)]
    return pairs


def per_device(wavefunction, env_left, right_environment_terms, source_tile_lookup):
    peers = lax.axis_size("sector")
    own = lax.axis_index("sector")
    tile_dev, terms, tile_rows = env_left.shape[0], env_left.shape[1], env_left.shape[2]
    rows, columns = wavefunction.shape
    shifts = source_tile_lookup.shape[1]
    records = tile_dev * shifts
    total = peers * rows * columns
    sizes = (tile_dev, shifts, terms // shifts, tile_rows, total)
    piece_rows = rows + STAT_ROWS
    lookup = source_tile_lookup
    own_records = lax.dynamic_slice_in_dim(lookup, own * tile_dev, tile_dev, 0).reshape(records)
    devices = jnp.arange(peers, dtype=jnp.int32)
    use_ring = peers * tile_dev <= 2 * records

    if use_ring:
        chips = peers // 2
        onward = ring_pairs(peers)
        sibling = [(i, i ^ 1) for i in range(peers)]
        half = chips // 2
        slots = [(p, rows) for p in range(peers)]
        first_list = second_list = own_records

        def swap_cores(x):
            return lax.ppermute(x, "sector", sibling)

        def step_on(x):
            return lax.ppermute(x, "sector", onward)

        def exchange(piece, contract, near):
            begins = near is None
            second = swap_cores(piece)
            order = list(range(4 * half - 4))
            left = []
            if near is None:
                first, second = lax.optimization_barrier((piece, second))
                near = prepare(second)
            else:
                first = piece
                left = [contract(0, piece, near, left)]
                left = [contract(1, second, near, left)]
                order = order[2:]
            pieces = [piece, second]
            for step in range(1, half):
                first = step_on(first)
                if step == 1 and not left:
                    first, counts = lax.optimization_barrier((first, near[2]))
                    near = (*near[:2], counts, *near[3:])
                pieces += [first, swap_cores(first)]
                second = step_on(second)
                pieces += [second, swap_cores(second)]
            first = step_on(first)
            for p in order:
                left = [contract(p, pieces[p], near, left)]
            first, left[0] = lax.optimization_barrier((first, left[0]))
            pieces += [first, swap_cores(first)]
            for p in range(4 * half - 4, 4 * half):
                more = [right_flat, wavefunction] if begins and p == 4 * half - 2 else []
                left = [contract(p, pieces[p], near, left, *more)]
            return pieces, near, left[0]

    else:
        capacity = max(1, 2 * records // peers)
        source = own_records // tile_dev
        local = own_records % tile_dev
        is_self = source == own
        hot = ((source[:, None] == devices[None, :]) & ~is_self[:, None]).astype(jnp.int32)
        rank = jnp.sum(hot * jnp.cumsum(hot, axis=0), axis=1) - 1
        every = lookup.reshape(peers, records)
        wanted = ((every // tile_dev == own) & (devices != own)[:, None]).astype(jnp.int32)
        order = jnp.cumsum(wanted, axis=1) - 1
        slots = jnp.arange(capacity, dtype=jnp.int32)
        chosen = wanted[:, :, None] * (order[:, :, None] == slots).astype(jnp.int32)
        send_index = jnp.sum(chosen * (every % tile_dev)[:, :, None], axis=1).reshape(-1)
        place = jnp.where(is_self, local, tile_dev + source * capacity + rank)
        first_list, second_list = jnp.zeros_like(source), place * tile_rows
        stat_base = (tile_dev + peers * capacity) * tile_rows
        slots = [(0, stat_base + d * STAT_ROWS) for d in range(peers)]

        def exchange(piece, contract, near):
            tiles = piece[:rows].reshape(tile_dev, tile_rows, columns)
            incoming = lax.all_to_all(tiles[send_index], "sector", 0, 0, tiled=True)
            stats = lax.all_gather(piece[rows:], "sector", axis=0, tiled=True)
            buffer = jnp.concatenate([piece[:rows], incoming.reshape(-1, columns), stats], axis=0)
            near = prepare(piece) if near is None else near
            return [buffer], near, contract(0, buffer, near, [])

    vmem = pl.BlockSpec(memory_space=pltpu.VMEM)
    smem = pl.BlockSpec(memory_space=pltpu.SMEM)
    hbm = pl.BlockSpec(memory_space=pltpu.HBM)

    piece = pl.pallas_call(
        start_kernel,
        out_shape=jax.ShapeDtypeStruct((piece_rows, columns), bf16),
        in_specs=[vmem],
        out_specs=vmem,
        compiler_params=pltpu.CompilerParams(vmem_limit_bytes=4 * 2**20),
    )(wavefunction)
    phases = max(p for p, _ in slots) + 1
    env_flat = env_left.reshape(tile_dev * terms * tile_rows, tile_rows)
    right_flat = right_environment_terms.reshape(terms * columns, columns)
    left_type = pltpu.VMEM((shifts * rows, (terms // shifts) * columns), bf16)

    def prepare(marker):
        tied = lax.optimization_barrier((own, first_list, second_list, env_flat, marker))
        counts, lists, places, env_near = pl.pallas_call(
            functools.partial(prepare_kernel, sizes, phases, peers, use_ring),
            out_shape=(
                pltpu.SMEM((phases,), jnp.int32),
                pltpu.SMEM((3, phases * records), jnp.int32),
                pltpu.SMEM((peers,), jnp.int32),
                pltpu.VMEM(env_flat.shape, bf16),
            ),
            in_specs=[smem, hbm, hbm, hbm],
            out_specs=(smem, smem, smem, vmem),
            scratch_shapes=[
                pltpu.SMEM((records,), jnp.int32),
                pltpu.SMEM((records,), jnp.int32),
                pltpu.SemaphoreType.DMA((3,)),
            ],
            compiler_params=pltpu.CompilerParams(vmem_limit_bytes=40 * 2**20),
        )(tied[0].reshape(1), *tied[1:4])
        return env_near, right_flat, counts, lists, places

    def contract(phase, buffer, near, held, *more):
        env_near, right_near, counts, lists, places = near
        return pl.pallas_call(
            functools.partial(left_kernel, phase, 10 if phase > peers - 3 else 5, sizes),
            out_shape=left_type,
            in_specs=[smem, smem] + [vmem] * (2 + len(held) + len(more)),
            out_specs=vmem,
            input_output_aliases={4: 0} if held else {},
            compiler_params=pltpu.CompilerParams(vmem_limit_bytes=4 * 2**20),
            cost_estimate=pl.CostEstimate(
                flops=2**32 if phase == 0 and not held else 2**29,
                bytes_accessed=2**20,
                transcendentals=0,
            ),
        )(counts, lists, buffer, env_near, *held, *more)

    def apply_operator(stage, buffers, near, held, prior, coefs):
        image = pltpu.VMEM((rows, columns), f32)
        small = jax.ShapeDtypeStruct((8, 128), f32)
        send = small if stage == 3 else jax.ShapeDtypeStruct((piece_rows, columns), bf16)
        env_near, right_near, counts, lists, places = near
        operands = [right_near, wavefunction, *buffers, *prior, *coefs, held]
        return pl.pallas_call(
            functools.partial(apply_kernel, stage, sizes, slots),
            out_shape=(image, small, send),
            in_specs=[smem] + [vmem] * len(operands),
            out_specs=(vmem, vmem, vmem),
            scratch_shapes=[pltpu.VMEM((peers * STAT_ROWS, 128), bf16)],
            compiler_params=pltpu.CompilerParams(vmem_limit_bytes=12 * 2**20),
            cost_estimate=pl.CostEstimate(
                flops=4 * rows * terms * tile_rows * columns, bytes_accessed=2**24, transcendentals=0
            ),
        )(places, *operands)

    buffers, near, left = exchange(piece, contract, None)
    image_one, coefs_one, piece = apply_operator(1, buffers, near, left, [], [])
    buffers, near, left = exchange(piece, contract, near)
    image_two, coefs_two, piece = apply_operator(2, buffers, near, left, [image_one], [coefs_one])
    buffers, near, left = exchange(piece, contract, near)
    image_three, coefs_three, stats = apply_operator(
        3, buffers, near, left, [image_one, image_two], [coefs_two]
    )
    distance = 1
    while distance < peers:
        pairs = [(i, i ^ distance) for i in range(peers)]
        stats = stats + lax.ppermute(stats, "sector", pairs)
        distance *= 2
    projected = pl.pallas_call(
        functools.partial(finish_kernel, total),
        out_shape=jax.ShapeDtypeStruct((3, 3), f32),
        in_specs=[vmem, vmem],
        out_specs=vmem,
        compiler_params=pltpu.CompilerParams(vmem_limit_bytes=2 * 2**20),
    )(stats, coefs_three)
    return (image_three, projected)


def solution(mesh):
    return jax.shard_map(
        per_device,
        mesh=mesh,
        in_specs=(
            P(("groups", "sector"), None),
            P(("groups", "sector"), None, None, None),
            P("groups", None, None),
            P("groups", None),
        ),
        out_specs=(P(("groups", "sector"), None), P("groups", None)),
        check_vma=False,
    )
```

profile of v0, /device:TPU:0, one launch (start us, length us, event | category | flops | bytes accessed | tf_op | source)
XLA Modules:
  0.0 113.0 jit_solution(12867009551099757150)
XLA Ops:
  0.7 0.9 copy-done.3
  2.3 1.2 %collective-permute-done.buf_ref.rest_1_ = bf16[1040,128]{1,0:T(8,128)(2,1)S(1)} collective-permute-done((bf16[1040,128]{1,0:T(8,128)(2,1)S(1)}, bf16[1040,128]{1,0:T(8,128)(2,1)S(1)}, u32[]{:S(2)}, u32[]{:S(2)}) %collective-permute-start) | collective-permute-done | bytes 266272 | tf_op jit(solution)/shard_map/ppermute | solution.py:268
  3.5 2.9 %collective-permute-start.1 = (bf16[1040,128]{1,0:T(8,128)(2,1)S(1)}, bf16[1040,128]{1,0:T(8,128)(2,1)S(1)}, u32[]{:S(2)}, u32[]{:S(2)}) collective-permute-start(bf16[1040,128]{1,0:T(8,128)(2,1)S(1)} %shard_map.59.buf_ref.rest_0_), channel_id=1, source_target_pairs={{0,4},{5,1},{4,8},{9,5},{8,12},{13,9},{12,14},{15,13},{14,10},{11,... | collective-permute-start | bytes 798728 | tf_op jit(solution)/shard_map/ppermute | solution.py:271
  6.6 1.6 %collective-permute-start.3 = (bf16[1040,128]{1,0:T(8,128)(2,1)S(1)}, bf16[1040,128]{1,0:T(8,128)(2,1)S(1)}, u32[]{:S(2)}, u32[]{:S(2)}) collective-permute-start(bf16[1040,128]{1,0:T(8,128)(2,1)S(1)} %collective-permute-done.buf_ref.rest_1_), channel_id=1, source_target_pairs={{0,4},{5,1},{4,8},{9,5},{8,12},{13,9},{12,14},{15,13},{14,10},{11,... | collective-permute-start | bytes 798728 | tf_op jit(solution)/shard_map/ppermute | solution.py:271
  8.2 4.0 %shard_map.60 = (s32[16]{0:T(128)S(4)}, s32[3,1280]{1,0:T(4,128)S(4)}, s32[16]{0:T(128)S(4)}, bf16[40960,128]{1,0:T(8,128)(2,1)S(1)}) custom-call(s32[1]{0:T(128)} %bitcast.1.own_ref, s32[80]{0:T(128)S(1)} %reshape.16.first_ref.second_ref, s32[80]{0:T(128)S(1)} %reshape.16.first_ref.second_ref, bf16[40960,128]{1,0:T(8,128)(2,1)} %bitcast.7), custom_call_target="tpu_custom_call" | custom-call | tf_op jit(solution)/shard_map/pallas_call | solution.py:349
  12.3 1.6 %collective-permute-start.5 = (bf16[1040,128]{1,0:T(8,128)(2,1)S(1)}, bf16[1040,128]{1,0:T(8,128)(2,1)S(1)}, u32[]{:S(2)}, u32[]{:S(2)}) collective-permute-start(bf16[1040,128]{1,0:T(8,128)(2,1)S(1)} %collective-permute-done.1.buf_ref.rest_2_), channel_id=1, source_target_pairs={{0,4},{5,1},{4,8},{9,5},{8,12},{13,9},{12,14},{15,13},{14,10},{11,... | collective-permute-start | bytes 798728 | tf_op jit(solution)/shard_map/ppermute | solution.py:271
  13.9 1.8 %collective-permute-start.7 = (bf16[1040,128]{1,0:T(8,128)(2,1)S(1)}, bf16[1040,128]{1,0:T(8,128)(2,1)S(1)}, u32[]{:S(2)}, u32[]{:S(2)}) collective-permute-start(bf16[1040,128]{1,0:T(8,128)(2,1)S(1)} %collective-permute-done.3.buf_ref.rest_4_), channel_id=1, source_target_pairs={{0,4},{5,1},{4,8},{9,5},{8,12},{13,9},{12,14},{15,13},{14,10},{11,... | collective-permute-start | bytes 798728 | tf_op jit(solution)/shard_map/ppermute | solution.py:271
  15.7 3.1 %collective-permute-done.5.buf_ref.rest_6_ = bf16[1040,128]{1,0:T(8,128)(2,1)S(1)} collective-permute-done((bf16[1040,128]{1,0:T(8,128)(2,1)S(1)}, bf16[1040,128]{1,0:T(8,128)(2,1)S(1)}, u32[]{:S(2)}, u32[]{:S(2)}) %collective-permute-start.5) | collective-permute-done | bytes 266272 | tf_op jit(solution)/shard_map/ppermute | solution.py:271
  18.7 1.6 %collective-permute-start.9 = (bf16[1040,128]{1,0:T(8,128)(2,1)S(1)}, bf16[1040,128]{1,0:T(8,128)(2,1)S(1)}, u32[]{:S(2)}, u32[]{:S(2)}) collective-permute-start(bf16[1040,128]{1,0:T(8,128)(2,1)S(1)} %collective-permute-done.5.buf_ref.rest_6_), channel_id=1, source_target_pairs={{0,4},{5,1},{4,8},{9,5},{8,12},{13,9},{12,14},{15,13},{14,10},{11,... | collective-permute-start | bytes 798728 | tf_op jit(solution)/shard_map/ppermute | solution.py:271
  21.6 1.6 %collective-permute-start.11 = (bf16[1040,128]{1,0:T(8,128)(2,1)S(1)}, bf16[1040,128]{1,0:T(8,128)(2,1)S(1)}, u32[]{:S(2)}, u32[]{:S(2)}) collective-permute-start(bf16[1040,128]{1,0:T(8,128)(2,1)S(1)} %collective-permute-done.7.buf_ref.rest_8_), channel_id=1, source_target_pairs={{0,4},{5,1},{4,8},{9,5},{8,12},{13,9},{12,14},{15,13},{14,10},{11,... | collective-permute-start | bytes 798728 | tf_op jit(solution)/shard_map/ppermute | solution.py:271
  26.2 1.3 %collective-permute-start.13 = (bf16[1040,128]{1,0:T(8,128)(2,1)S(1)}, bf16[1040,128]{1,0:T(8,128)(2,1)S(1)}, u32[]{:S(2)}, u32[]{:S(2)}) collective-permute-start(bf16[1040,128]{1,0:T(8,128)(2,1)S(1)} %collective-permute-done.9.buf_ref.rest_10_), channel_id=1, source_target_pairs={{0,4},{5,1},{4,8},{9,5},{8,12},{13,9},{12,14},{15,13},{14,10},{11,... | collective-permute-start | bytes 798728 | tf_op jit(solution)/shard_map/ppermute | solution.py:271
  30.2 2.5 %collective-permute-done.13.buf_ref.rest_14_ = bf16[1040,128]{1,0:T(8,128)(2,1)S(1)} collective-permute-done((bf16[1040,128]{1,0:T(8,128)(2,1)S(1)}, bf16[1040,128]{1,0:T(8,128)(2,1)S(1)}, u32[]{:S(2)}, u32[]{:S(2)}) %collective-permute-start.13) | collective-permute-done | bytes 266272 | tf_op jit(solution)/shard_map/ppermute | solution.py:271
  34.2 2.9 %shard_map.77 = (f32[1024,128]{1,0:T(8,128)S(1)}, f32[8,128]{1,0:T(8,128)S(1)}, bf16[1040,128]{1,0:T(8,128)(2,1)S(1)}) custom-call(s32[16]{0:T(128)S(4)} %get-tuple-element.34.stat_ref, bf16[5120,128]{1,0:T(8,128)(2,1)S(1)} %bitcast.4, bf16[1024,128]{1,0:T(8,128)(2,1)S(1)} %copy-done.4, bf16[1040,128]{1,0:T(8,128)(2,1)S(1)} %shard_map.59.buf_ref.rest_0_, ...), custom_call_target="tpu_custom_call" | custom-call | flops 2684354560 | bytes 16777216 | tf_op jit(solution)/shard_map/pallas_call | solution.py:390
  37.1 0.9 collective-permute-start.15
  38.0 1.3 %collective-permute-start.16 = (bf16[1040,128]{1,0:T(8,128)(2,1)S(1)}, bf16[1040,128]{1,0:T(8,128)(2,1)S(1)}, u32[]{:S(2)}, u32[]{:S(2)}) collective-permute-start(bf16[1040,128]{1,0:T(8,128)(2,1)S(1)} %get-tuple-element.43.buf_ref.rest_0_), channel_id=1, source_target_pairs={{0,4},{5,1},{4,8},{9,5},{8,12},{13,9},{12,14},{15,13},{14,10},{11,... | collective-permute-start | bytes 798728 | tf_op jit(solution)/shard_map/ppermute | solution.py:271
  39.3 2.0 %collective-permute-start.18 = (bf16[1040,128]{1,0:T(8,128)(2,1)S(1)}, bf16[1040,128]{1,0:T(8,128)(2,1)S(1)}, u32[]{:S(2)}, u32[]{:S(2)}) collective-permute-start(bf16[1040,128]{1,0:T(8,128)(2,1)S(1)} %collective-permute-done.15.buf_ref.rest_1_), channel_id=1, source_target_pairs={{0,4},{5,1},{4,8},{9,5},{8,12},{13,9},{12,14},{15,13},{14,10},{11,... | collective-permute-start | bytes 798728 | tf_op jit(solution)/shard_map/ppermute | solution.py:271
  41.3 3.2 %collective-permute-done.16.buf_ref.rest_2_ = bf16[1040,128]{1,0:T(8,128)(2,1)S(1)} collective-permute-done((bf16[1040,128]{1,0:T(8,128)(2,1)S(1)}, bf16[1040,128]{1,0:T(8,128)(2,1)S(1)}, u32[]{:S(2)}, u32[]{:S(2)}) %collective-permute-start.16) | collective-permute-done | bytes 266272 | tf_op jit(solution)/shard_map/ppermute | solution.py:271
  44.4 1.3 %collective-permute-start.20 = (bf16[1040,128]{1,0:T(8,128)(2,1)S(1)}, bf16[1040,128]{1,0:T(8,128)(2,1)S(1)}, u32[]{:S(2)}, u32[]{:S(2)}) collective-permute-start(bf16[1040,128]{1,0:T(8,128)(2,1)S(1)} %collective-permute-done.16.buf_ref.rest_2_), channel_id=1, source_target_pairs={{0,4},{5,1},{4,8},{9,5},{8,12},{13,9},{12,14},{15,13},{14,10},{11,... | collective-permute-start | bytes 798728 | tf_op jit(solution)/shard_map/ppermute | solution.py:271
  45.7 1.5 %collective-permute-done.18.buf_ref.rest_4_ = bf16[1040,128]{1,0:T(8,128)(2,1)S(1)} collective-permute-done((bf16[1040,128]{1,0:T(8,128)(2,1)S(1)}, bf16[1040,128]{1,0:T(8,128)(2,1)S(1)}, u32[]{:S(2)}, u32[]{:S(2)}) %collective-permute-start.18) | collective-permute-done | bytes 266272 | tf_op jit(solution)/shard_map/ppermute | solution.py:271
  47.3 1.3 %collective-permute-start.22 = (bf16[1040,128]{1,0:T(8,128)(2,1)S(1)}, bf16[1040,128]{1,0:T(8,128)(2,1)S(1)}, u32[]{:S(2)}, u32[]{:S(2)}) collective-permute-start(bf16[1040,128]{1,0:T(8,128)(2,1)S(1)} %collective-permute-done.18.buf_ref.rest_4_), channel_id=1, source_target_pairs={{0,4},{5,1},{4,8},{9,5},{8,12},{13,9},{12,14},{15,13},{14,10},{11,... | collective-permute-start | bytes 798728 | tf_op jit(solution)/shard_map/ppermute | solution.py:271
  48.6 2.3 %collective-permute-done.20.buf_ref.rest_6_ = bf16[1040,128]{1,0:T(8,128)(2,1)S(1)} collective-permute-done((bf16[1040,128]{1,0:T(8,128)(2,1)S(1)}, bf16[1040,128]{1,0:T(8,128)(2,1)S(1)}, u32[]{:S(2)}, u32[]{:S(2)}) %collective-permute-start.20) | collective-permute-done | bytes 266272 | tf_op jit(solution)/shard_map/ppermute | solution.py:271
  50.8 1.3 %collective-permute-start.24 = (bf16[1040,128]{1,0:T(8,128)(2,1)S(1)}, bf16[1040,128]{1,0:T(8,128)(2,1)S(1)}, u32[]{:S(2)}, u32[]{:S(2)}) collective-permute-start(bf16[1040,128]{1,0:T(8,128)(2,1)S(1)} %collective-permute-done.20.buf_ref.rest_6_), channel_id=1, source_target_pairs={{0,4},{5,1},{4,8},{9,5},{8,12},{13,9},{12,14},{15,13},{14,10},{11,... | collective-permute-start | bytes 798728 | tf_op jit(solution)/shard_map/ppermute | solution.py:271
  53.9 1.0 collective-permute-start.26
  55.7 1.6 %collective-permute-done.24.buf_ref.rest_10_ = bf16[1040,128]{1,0:T(8,128)(2,1)S(1)} collective-permute-done((bf16[1040,128]{1,0:T(8,128)(2,1)S(1)}, bf16[1040,128]{1,0:T(8,128)(2,1)S(1)}, u32[]{:S(2)}, u32[]{:S(2)}) %collective-permute-start.24) | collective-permute-done | bytes 266272 | tf_op jit(solution)/shard_map/ppermute | solution.py:271
  57.2 1.3 %collective-permute-start.28 = (bf16[1040,128]{1,0:T(8,128)(2,1)S(1)}, bf16[1040,128]{1,0:T(8,128)(2,1)S(1)}, u32[]{:S(2)}, u32[]{:S(2)}) collective-permute-start(bf16[1040,128]{1,0:T(8,128)(2,1)S(1)} %collective-permute-done.24.buf_ref.rest_10_), channel_id=1, source_target_pairs={{0,4},{5,1},{4,8},{9,5},{8,12},{13,9},{12,14},{15,13},{14,10},{11,... | collective-permute-start | bytes 798728 | tf_op jit(solution)/shard_map/ppermute | solution.py:271
  61.8 1.8 %collective-permute-done.28.buf_ref.rest_14_ = bf16[1040,128]{1,0:T(8,128)(2,1)S(1)} collective-permute-done((bf16[1040,128]{1,0:T(8,128)(2,1)S(1)}, bf16[1040,128]{1,0:T(8,128)(2,1)S(1)}, u32[]{:S(2)}, u32[]{:S(2)}) %collective-permute-start.28) | collective-permute-done | bytes 266272 | tf_op jit(solution)/shard_map/ppermute | solution.py:271
  64.4 0.8 collective-permute-done.29.buf_ref.rest_15_
  65.2 2.9 %shard_map.94 = (f32[1024,128]{1,0:T(8,128)S(1)}, f32[8,128]{1,0:T(8,128)S(1)}, bf16[1040,128]{1,0:T(8,128)(2,1)S(1)}) custom-call(s32[16]{0:T(128)S(4)} %get-tuple-element.34.stat_ref, bf16[5120,128]{1,0:T(8,128)(2,1)S(1)} %bitcast.5, bf16[1024,128]{1,0:T(8,128)(2,1)S(1)} %copy-done.4, bf16[1040,128]{1,0:T(8,128)(2,1)S(1)} %get-tuple-element.43.buf_ref.rest_0_, ...), custom_call_target="tpu_custom_call" | custom-call | flops 2684354560 | bytes 16777216 | tf_op jit(solution)/shard_map/pallas_call | solution.py:390
  68.8 1.3 %collective-permute-start.31 = (bf16[1040,128]{1,0:T(8,128)(2,1)S(1)}, bf16[1040,128]{1,0:T(8,128)(2,1)S(1)}, u32[]{:S(2)}, u32[]{:S(2)}) collective-permute-start(bf16[1040,128]{1,0:T(8,128)(2,1)S(1)} %get-tuple-element.48.buf_ref.rest_0_), channel_id=1, source_target_pairs={{0,4},{5,1},{4,8},{9,5},{8,12},{13,9},{12,14},{15,13},{14,10},{11,... | collective-permute-start | bytes 798728 | tf_op jit(solution)/shard_map/ppermute | solution.py:271
  70.1 2.1 %collective-permute-start.33 = (bf16[1040,128]{1,0:T(8,128)(2,1)S(1)}, bf16[1040,128]{1,0:T(8,128)(2,1)S(1)}, u32[]{:S(2)}, u32[]{:S(2)}) collective-permute-start(bf16[1040,128]{1,0:T(8,128)(2,1)S(1)} %collective-permute-done.30.buf_ref.rest_1_), channel_id=1, source_target_pairs={{0,4},{5,1},{4,8},{9,5},{8,12},{13,9},{12,14},{15,13},{14,10},{11,... | collective-permute-start | bytes 798728 | tf_op jit(solution)/shard_map/ppermute | solution.py:271
  72.2 3.1 %collective-permute-done.31.buf_ref.rest_2_ = bf16[1040,128]{1,0:T(8,128)(2,1)S(1)} collective-permute-done((bf16[1040,128]{1,0:T(8,128)(2,1)S(1)}, bf16[1040,128]{1,0:T(8,128)(2,1)S(1)}, u32[]{:S(2)}, u32[]{:S(2)}) %collective-permute-start.31) | collective-permute-done | bytes 266272 | tf_op jit(solution)/shard_map/ppermute | solution.py:271
  75.2 1.3 %collective-permute-start.35 = (bf16[1040,128]{1,0:T(8,128)(2,1)S(1)}, bf16[1040,128]{1,0:T(8,128)(2,1)S(1)}, u32[]{:S(2)}, u32[]{:S(2)}) collective-permute-start(bf16[1040,128]{1,0:T(8,128)(2,1)S(1)} %collective-permute-done.31.buf_ref.rest_2_), channel_id=1, source_target_pairs={{0,4},{5,1},{4,8},{9,5},{8,12},{13,9},{12,14},{15,13},{14,10},{11,... | collective-permute-start | bytes 798728 | tf_op jit(solution)/shard_map/ppermute | solution.py:271
  76.5 1.6 %collective-permute-done.33.buf_ref.rest_4_ = bf16[1040,128]{1,0:T(8,128)(2,1)S(1)} collective-permute-done((bf16[1040,128]{1,0:T(8,128)(2,1)S(1)}, bf16[1040,128]{1,0:T(8,128)(2,1)S(1)}, u32[]{:S(2)}, u32[]{:S(2)}) %collective-permute-start.33) | collective-permute-done | bytes 266272 | tf_op jit(solution)/shard_map/ppermute | solution.py:271
  78.1 1.3 %collective-permute-start.37 = (bf16[1040,128]{1,0:T(8,128)(2,1)S(1)}, bf16[1040,128]{1,0:T(8,128)(2,1)S(1)}, u32[]{:S(2)}, u32[]{:S(2)}) collective-permute-start(bf16[1040,128]{1,0:T(8,128)(2,1)S(1)} %collective-permute-done.33.buf_ref.rest_4_), channel_id=1, source_target_pairs={{0,4},{5,1},{4,8},{9,5},{8,12},{13,9},{12,14},{15,13},{14,10},{11,... | collective-permute-start | bytes 798728 | tf_op jit(solution)/shard_map/ppermute | solution.py:271
  79.4 2.3 %collective-permute-done.35.buf_ref.rest_6_ = bf16[1040,128]{1,0:T(8,128)(2,1)S(1)} collective-permute-done((bf16[1040,128]{1,0:T(8,128)(2,1)S(1)}, bf16[1040,128]{1,0:T(8,128)(2,1)S(1)}, u32[]{:S(2)}, u32[]{:S(2)}) %collective-permute-start.35) | collective-permute-done | bytes 266272 | tf_op jit(solution)/shard_map/ppermute | solution.py:271
  81.6 1.3 %collective-permute-start.39 = (bf16[1040,128]{1,0:T(8,128)(2,1)S(1)}, bf16[1040,128]{1,0:T(8,128)(2,1)S(1)}, u32[]{:S(2)}, u32[]{:S(2)}) collective-permute-start(bf16[1040,128]{1,0:T(8,128)(2,1)S(1)} %collective-permute-done.35.buf_ref.rest_6_), channel_id=1, source_target_pairs={{0,4},{5,1},{4,8},{9,5},{8,12},{13,9},{12,14},{15,13},{14,10},{11,... | collective-permute-start | bytes 798728 | tf_op jit(solution)/shard_map/ppermute | solution.py:271
  84.7 1.1 collective-permute-start.41
  86.5 1.5 %collective-permute-done.39.buf_ref.rest_10_ = bf16[1040,128]{1,0:T(8,128)(2,1)S(1)} collective-permute-done((bf16[1040,128]{1,0:T(8,128)(2,1)S(1)}, bf16[1040,128]{1,0:T(8,128)(2,1)S(1)}, u32[]{:S(2)}, u32[]{:S(2)}) %collective-permute-start.39) | collective-permute-done | bytes 266272 | tf_op jit(solution)/shard_map/ppermute | solution.py:271
  88.1 1.3 %collective-permute-start.43 = (bf16[1040,128]{1,0:T(8,128)(2,1)S(1)}, bf16[1040,128]{1,0:T(8,128)(2,1)S(1)}, u32[]{:S(2)}, u32[]{:S(2)}) collective-permute-start(bf16[1040,128]{1,0:T(8,128)(2,1)S(1)} %collective-permute-done.39.buf_ref.rest_10_), channel_id=1, source_target_pairs={{0,4},{5,1},{4,8},{9,5},{8,12},{13,9},{12,14},{15,13},{14,10},{11,... | collective-permute-start | bytes 798728 | tf_op jit(solution)/shard_map/ppermute | solution.py:271
  92.6 1.9 %collective-permute-done.43.buf_ref.rest_14_ = bf16[1040,128]{1,0:T(8,128)(2,1)S(1)} collective-permute-done((bf16[1040,128]{1,0:T(8,128)(2,1)S(1)}, bf16[1040,128]{1,0:T(8,128)(2,1)S(1)}, u32[]{:S(2)}, u32[]{:S(2)}) %collective-permute-start.43) | collective-permute-done | bytes 266272 | tf_op jit(solution)/shard_map/ppermute | solution.py:271
  95.2 0.8 collective-permute-done.44.buf_ref.rest_15_
  96.0 3.0 %shard_map.111 = (f32[1024,128]{1,0:T(8,128)S(1)}, f32[8,128]{1,0:T(8,128)S(1)}, f32[8,128]{1,0:T(8,128)S(1)}) custom-call(s32[16]{0:T(128)S(4)} %get-tuple-element.34.stat_ref, bf16[5120,128]{1,0:T(8,128)(2,1)S(1)} %bitcast.6, bf16[1024,128]{1,0:T(8,128)(2,1)S(1)} %copy-done.4, bf16[1040,128]{1,0:T(8,128)(2,1)S(1)} %get-tuple-element.48.buf_ref.rest_0_, ...), custom_call_target="tpu_custom_call" | custom-call | flops 2684354560 | bytes 16777216 | tf_op jit(solution)/shard_map/pallas_call | solution.py:390
  99.7 0.8 collective-permute-done.45
  101.2 2.9 %collective-permute-done.46 = f32[8,128]{1,0:T(8,128)S(1)} collective-permute-done((f32[8,128]{1,0:T(8,128)S(1)}, f32[8,128]{1,0:T(8,128)S(1)}, u32[]{:S(2)}, u32[]{:S(2)}) %collective-permute-start.46) | collective-permute-done | bytes 4128 | tf_op jit(solution)/shard_map/ppermute | solution.py:413
  104.1 1.7 %collective-permute-start.47 = (f32[8,128]{1,0:T(8,128)S(1)}, f32[8,128]{1,0:T(8,128)S(1)}, u32[]{:S(2)}, u32[]{:S(2)}) collective-permute-start(f32[8,128]{1,0:T(8,128)S(1)} %add.17), channel_id=1, source_target_pairs={{0,4},{1,5},{2,6},{3,7},{4,0},{5,1},{6,2},{7,3},{8,12},{9,13},{10,... | collective-permute-start | bytes 12296 | tf_op jit(solution)/shard_map/ppermute | solution.py:413
  105.8 2.0 %collective-permute-done.47 = f32[8,128]{1,0:T(8,128)S(1)} collective-permute-done((f32[8,128]{1,0:T(8,128)S(1)}, f32[8,128]{1,0:T(8,128)S(1)}, u32[]{:S(2)}, u32[]{:S(2)}) %collective-permute-start.47) | collective-permute-done | bytes 4128 | tf_op jit(solution)/shard_map/ppermute | solution.py:413
  107.7 3.0 %collective-permute-start.48 = (f32[8,128]{1,0:T(8,128)S(1)}, f32[8,128]{1,0:T(8,128)S(1)}, u32[]{:S(2)}, u32[]{:S(2)}) collective-permute-start(f32[8,128]{1,0:T(8,128)S(1)} %add.18), channel_id=1, source_target_pairs={{0,8},{1,9},{2,10},{3,11},{4,12},{5,13},{6,14},{7,15},{8,0},{9,1},... | collective-permute-start | bytes 12296 | tf_op jit(solution)/shard_map/ppermute | solution.py:413
  110.7 0.8 copy.97
  (122 shorter events, 25.7 us)
Async XLA Ops:
  1.8 1.7 %collective-permute-start = (bf16[1040,128]{1,0:T(8,128)(2,1)S(1)}, bf16[1040,128]{1,0:T(8,128)(2,1)S(1)}, u32[]{:S(2)}, u32[]{:S(2)}) collective-permute-start(bf16[1040,128]{1,0:T(8,128)(2,1)S(1)} %shard_map.59.buf_ref.rest_0_), channel_id=1, source_target_pairs={{0,1},{1,0},{2,3},{3,2},{4,5},{5,4},{6,7},{7,6},{8,9},{9,8},{10,11... | collective-permute-start | bytes 798728 | tf_op jit(solution)/shard_map/ppermute | solution.py:268
  3.5 8.8 %collective-permute-start.1 = (bf16[1040,128]{1,0:T(8,128)(2,1)S(1)}, bf16[1040,128]{1,0:T(8,128)(2,1)S(1)}, u32[]{:S(2)}, u32[]{:S(2)}) collective-permute-start(bf16[1040,128]{1,0:T(8,128)(2,1)S(1)} %shard_map.59.buf_ref.rest_0_), channel_id=1, source_target_pairs={{0,4},{5,1},{4,8},{9,5},{8,12},{13,9},{12,14},{15,13},{14,10},{11,... | collective-permute-start | bytes 798728 | tf_op jit(solution)/shard_map/ppermute | solution.py:271
  6.6 7.3 %collective-permute-start.3 = (bf16[1040,128]{1,0:T(8,128)(2,1)S(1)}, bf16[1040,128]{1,0:T(8,128)(2,1)S(1)}, u32[]{:S(2)}, u32[]{:S(2)}) collective-permute-start(bf16[1040,128]{1,0:T(8,128)(2,1)S(1)} %collective-permute-done.buf_ref.rest_1_), channel_id=1, source_target_pairs={{0,4},{5,1},{4,8},{9,5},{8,12},{13,9},{12,14},{15,13},{14,10},{11,... | collective-permute-start | bytes 798728 | tf_op jit(solution)/shard_map/ppermute | solution.py:271
  12.3 6.5 %collective-permute-start.5 = (bf16[1040,128]{1,0:T(8,128)(2,1)S(1)}, bf16[1040,128]{1,0:T(8,128)(2,1)S(1)}, u32[]{:S(2)}, u32[]{:S(2)}) collective-permute-start(bf16[1040,128]{1,0:T(8,128)(2,1)S(1)} %collective-permute-done.1.buf_ref.rest_2_), channel_id=1, source_target_pairs={{0,4},{5,1},{4,8},{9,5},{8,12},{13,9},{12,14},{15,13},{14,10},{11,... | collective-permute-start | bytes 798728 | tf_op jit(solution)/shard_map/ppermute | solution.py:271
  13.9 10.3 %collective-permute-start.2 = (bf16[1040,128]{1,0:T(8,128)(2,1)S(1)}, bf16[1040,128]{1,0:T(8,128)(2,1)S(1)}, u32[]{:S(2)}, u32[]{:S(2)}) collective-permute-start(bf16[1040,128]{1,0:T(8,128)(2,1)S(1)} %collective-permute-done.1.buf_ref.rest_2_), channel_id=1, source_target_pairs={{0,1},{1,0},{2,3},{3,2},{4,5},{5,4},{6,7},{7,6},{8,9},{9,8},{10,11... | collective-permute-start | bytes 798728 | tf_op jit(solution)/shard_map/ppermute | solution.py:268
  13.9 7.7 %collective-permute-start.7 = (bf16[1040,128]{1,0:T(8,128)(2,1)S(1)}, bf16[1040,128]{1,0:T(8,128)(2,1)S(1)}, u32[]{:S(2)}, u32[]{:S(2)}) collective-permute-start(bf16[1040,128]{1,0:T(8,128)(2,1)S(1)} %collective-permute-done.3.buf_ref.rest_4_), channel_id=1, source_target_pairs={{0,4},{5,1},{4,8},{9,5},{8,12},{13,9},{12,14},{15,13},{14,10},{11,... | collective-permute-start | bytes 798728 | tf_op jit(solution)/shard_map/ppermute | solution.py:271
  15.7 9.9 %collective-permute-start.4 = (bf16[1040,128]{1,0:T(8,128)(2,1)S(1)}, bf16[1040,128]{1,0:T(8,128)(2,1)S(1)}, u32[]{:S(2)}, u32[]{:S(2)}) collective-permute-start(bf16[1040,128]{1,0:T(8,128)(2,1)S(1)} %collective-permute-done.3.buf_ref.rest_4_), channel_id=1, source_target_pairs={{0,1},{1,0},{2,3},{3,2},{4,5},{5,4},{6,7},{7,6},{8,9},{9,8},{10,11... | collective-permute-start | bytes 798728 | tf_op jit(solution)/shard_map/ppermute | solution.py:268
  18.7 6.4 %collective-permute-start.9 = (bf16[1040,128]{1,0:T(8,128)(2,1)S(1)}, bf16[1040,128]{1,0:T(8,128)(2,1)S(1)}, u32[]{:S(2)}, u32[]{:S(2)}) collective-permute-start(bf16[1040,128]{1,0:T(8,128)(2,1)S(1)} %collective-permute-done.5.buf_ref.rest_6_), channel_id=1, source_target_pairs={{0,4},{5,1},{4,8},{9,5},{8,12},{13,9},{12,14},{15,13},{14,10},{11,... | collective-permute-start | bytes 798728 | tf_op jit(solution)/shard_map/ppermute | solution.py:271
  21.0 7.0 %collective-permute-start.6 = (bf16[1040,128]{1,0:T(8,128)(2,1)S(1)}, bf16[1040,128]{1,0:T(8,128)(2,1)S(1)}, u32[]{:S(2)}, u32[]{:S(2)}) collective-permute-start(bf16[1040,128]{1,0:T(8,128)(2,1)S(1)} %collective-permute-done.5.buf_ref.rest_6_), channel_id=1, source_target_pairs={{0,1},{1,0},{2,3},{3,2},{4,5},{5,4},{6,7},{7,6},{8,9},{9,8},{10,11... | collective-permute-start | bytes 798728 | tf_op jit(solution)/shard_map/ppermute | solution.py:268
  21.6 6.4 %collective-permute-start.11 = (bf16[1040,128]{1,0:T(8,128)(2,1)S(1)}, bf16[1040,128]{1,0:T(8,128)(2,1)S(1)}, u32[]{:S(2)}, u32[]{:S(2)}) collective-permute-start(bf16[1040,128]{1,0:T(8,128)(2,1)S(1)} %collective-permute-done.7.buf_ref.rest_8_), channel_id=1, source_target_pairs={{0,4},{5,1},{4,8},{9,5},{8,12},{13,9},{12,14},{15,13},{14,10},{11,... | collective-permute-start | bytes 798728 | tf_op jit(solution)/shard_map/ppermute | solution.py:271
  24.2 4.5 %collective-permute-start.8 = (bf16[1040,128]{1,0:T(8,128)(2,1)S(1)}, bf16[1040,128]{1,0:T(8,128)(2,1)S(1)}, u32[]{:S(2)}, u32[]{:S(2)}) collective-permute-start(bf16[1040,128]{1,0:T(8,128)(2,1)S(1)} %collective-permute-done.7.buf_ref.rest_8_), channel_id=1, source_target_pairs={{0,1},{1,0},{2,3},{3,2},{4,5},{5,4},{6,7},{7,6},{8,9},{9,8},{10,11... | collective-permute-start | bytes 798728 | tf_op jit(solution)/shard_map/ppermute | solution.py:268
  25.2 4.3 %collective-permute-start.10 = (bf16[1040,128]{1,0:T(8,128)(2,1)S(1)}, bf16[1040,128]{1,0:T(8,128)(2,1)S(1)}, u32[]{:S(2)}, u32[]{:S(2)}) collective-permute-start(bf16[1040,128]{1,0:T(8,128)(2,1)S(1)} %collective-permute-done.9.buf_ref.rest_10_), channel_id=1, source_target_pairs={{0,1},{1,0},{2,3},{3,2},{4,5},{5,4},{6,7},{7,6},{8,9},{9,8},{10,11... | collective-permute-start | bytes 798728 | tf_op jit(solution)/shard_map/ppermute | solution.py:268
  26.2 6.5 %collective-permute-start.13 = (bf16[1040,128]{1,0:T(8,128)(2,1)S(1)}, bf16[1040,128]{1,0:T(8,128)(2,1)S(1)}, u32[]{:S(2)}, u32[]{:S(2)}) collective-permute-start(bf16[1040,128]{1,0:T(8,128)(2,1)S(1)} %collective-permute-done.9.buf_ref.rest_10_), channel_id=1, source_target_pairs={{0,4},{5,1},{4,8},{9,5},{8,12},{13,9},{12,14},{15,13},{14,10},{11,... | collective-permute-start | bytes 798728 | tf_op jit(solution)/shard_map/ppermute | solution.py:271
  28.0 4.7 %collective-permute-start.12 = (bf16[1040,128]{1,0:T(8,128)(2,1)S(1)}, bf16[1040,128]{1,0:T(8,128)(2,1)S(1)}, u32[]{:S(2)}, u32[]{:S(2)}) collective-permute-start(bf16[1040,128]{1,0:T(8,128)(2,1)S(1)} %collective-permute-done.11.buf_ref.rest_12_), channel_id=1, source_target_pairs={{0,1},{1,0},{2,3},{3,2},{4,5},{5,4},{6,7},{7,6},{8,9},{9,8},{10,11... | collective-permute-start | bytes 798728 | tf_op jit(solution)/shard_map/ppermute | solution.py:268
  32.7 1.5 %collective-permute-start.14 = (bf16[1040,128]{1,0:T(8,128)(2,1)S(1)}, bf16[1040,128]{1,0:T(8,128)(2,1)S(1)}, u32[]{:S(2)}, u32[]{:S(2)}) collective-permute-start(bf16[1040,128]{1,0:T(8,128)(2,1)S(1)} %collective-permute-done.13.buf_ref.rest_14_), channel_id=1, source_target_pairs={{0,1},{1,0},{2,3},{3,2},{4,5},{5,4},{6,7},{7,6},{8,9},{9,8},{10,11... | collective-permute-start | bytes 798728 | tf_op jit(solution)/shard_map/ppermute | solution.py:268
  37.1 2.2 %collective-permute-start.15 = (bf16[1040,128]{1,0:T(8,128)(2,1)S(1)}, bf16[1040,128]{1,0:T(8,128)(2,1)S(1)}, u32[]{:S(2)}, u32[]{:S(2)}) collective-permute-start(bf16[1040,128]{1,0:T(8,128)(2,1)S(1)} %get-tuple-element.43.buf_ref.rest_0_), channel_id=1, source_target_pairs={{0,1},{1,0},{2,3},{3,2},{4,5},{5,4},{6,7},{7,6},{8,9},{9,8},{10,11... | collective-permute-start | bytes 798728 | tf_op jit(solution)/shard_map/ppermute | solution.py:268
  38.0 6.4 %collective-permute-start.16 = (bf16[1040,128]{1,0:T(8,128)(2,1)S(1)}, bf16[1040,128]{1,0:T(8,128)(2,1)S(1)}, u32[]{:S(2)}, u32[]{:S(2)}) collective-permute-start(bf16[1040,128]{1,0:T(8,128)(2,1)S(1)} %get-tuple-element.43.buf_ref.rest_0_), channel_id=1, source_target_pairs={{0,4},{5,1},{4,8},{9,5},{8,12},{13,9},{12,14},{15,13},{14,10},{11,... | collective-permute-start | bytes 798728 | tf_op jit(solution)/shard_map/ppermute | solution.py:271
  39.3 8.0 %collective-permute-start.18 = (bf16[1040,128]{1,0:T(8,128)(2,1)S(1)}, bf16[1040,128]{1,0:T(8,128)(2,1)S(1)}, u32[]{:S(2)}, u32[]{:S(2)}) collective-permute-start(bf16[1040,128]{1,0:T(8,128)(2,1)S(1)} %collective-permute-done.15.buf_ref.rest_1_), channel_id=1, source_target_pairs={{0,4},{5,1},{4,8},{9,5},{8,12},{13,9},{12,14},{15,13},{14,10},{11,... | collective-permute-start | bytes 798728 | tf_op jit(solution)/shard_map/ppermute | solution.py:271
  44.4 6.4 %collective-permute-start.20 = (bf16[1040,128]{1,0:T(8,128)(2,1)S(1)}, bf16[1040,128]{1,0:T(8,128)(2,1)S(1)}, u32[]{:S(2)}, u32[]{:S(2)}) collective-permute-start(bf16[1040,128]{1,0:T(8,128)(2,1)S(1)} %collective-permute-done.16.buf_ref.rest_2_), channel_id=1, source_target_pairs={{0,4},{5,1},{4,8},{9,5},{8,12},{13,9},{12,14},{15,13},{14,10},{11,... | collective-permute-start | bytes 798728 | tf_op jit(solution)/shard_map/ppermute | solution.py:271
  45.7 9.3 %collective-permute-start.17 = (bf16[1040,128]{1,0:T(8,128)(2,1)S(1)}, bf16[1040,128]{1,0:T(8,128)(2,1)S(1)}, u32[]{:S(2)}, u32[]{:S(2)}) collective-permute-start(bf16[1040,128]{1,0:T(8,128)(2,1)S(1)} %collective-permute-done.16.buf_ref.rest_2_), channel_id=1, source_target_pairs={{0,1},{1,0},{2,3},{3,2},{4,5},{5,4},{6,7},{7,6},{8,9},{9,8},{10,11... | collective-permute-start | bytes 798728 | tf_op jit(solution)/shard_map/ppermute | solution.py:268
  47.3 6.7 %collective-permute-start.22 = (bf16[1040,128]{1,0:T(8,128)(2,1)S(1)}, bf16[1040,128]{1,0:T(8,128)(2,1)S(1)}, u32[]{:S(2)}, u32[]{:S(2)}) collective-permute-start(bf16[1040,128]{1,0:T(8,128)(2,1)S(1)} %collective-permute-done.18.buf_ref.rest_4_), channel_id=1, source_target_pairs={{0,4},{5,1},{4,8},{9,5},{8,12},{13,9},{12,14},{15,13},{14,10},{11,... | collective-permute-start | bytes 798728 | tf_op jit(solution)/shard_map/ppermute | solution.py:271
  48.6 10.0 %collective-permute-start.19 = (bf16[1040,128]{1,0:T(8,128)(2,1)S(1)}, bf16[1040,128]{1,0:T(8,128)(2,1)S(1)}, u32[]{:S(2)}, u32[]{:S(2)}) collective-permute-start(bf16[1040,128]{1,0:T(8,128)(2,1)S(1)} %collective-permute-done.18.buf_ref.rest_4_), channel_id=1, source_target_pairs={{0,1},{1,0},{2,3},{3,2},{4,5},{5,4},{6,7},{7,6},{8,9},{9,8},{10,11... | collective-permute-start | bytes 798728 | tf_op jit(solution)/shard_map/ppermute | solution.py:268
  50.8 6.4 %collective-permute-start.24 = (bf16[1040,128]{1,0:T(8,128)(2,1)S(1)}, bf16[1040,128]{1,0:T(8,128)(2,1)S(1)}, u32[]{:S(2)}, u32[]{:S(2)}) collective-permute-start(bf16[1040,128]{1,0:T(8,128)(2,1)S(1)} %collective-permute-done.20.buf_ref.rest_6_), channel_id=1, source_target_pairs={{0,4},{5,1},{4,8},{9,5},{8,12},{13,9},{12,14},{15,13},{14,10},{11,... | collective-permute-start | bytes 798728 | tf_op jit(solution)/shard_map/ppermute | solution.py:271
  52.8 6.6 %collective-permute-start.21 = (bf16[1040,128]{1,0:T(8,128)(2,1)S(1)}, bf16[1040,128]{1,0:T(8,128)(2,1)S(1)}, u32[]{:S(2)}, u32[]{:S(2)}) collective-permute-start(bf16[1040,128]{1,0:T(8,128)(2,1)S(1)} %collective-permute-done.20.buf_ref.rest_6_), channel_id=1, source_target_pairs={{0,1},{1,0},{2,3},{3,2},{4,5},{5,4},{6,7},{7,6},{8,9},{9,8},{10,11... | collective-permute-start | bytes 798728 | tf_op jit(solution)/shard_map/ppermute | solution.py:268
  53.9 6.5 %collective-permute-start.26 = (bf16[1040,128]{1,0:T(8,128)(2,1)S(1)}, bf16[1040,128]{1,0:T(8,128)(2,1)S(1)}, u32[]{:S(2)}, u32[]{:S(2)}) collective-permute-start(bf16[1040,128]{1,0:T(8,128)(2,1)S(1)} %collective-permute-done.22.buf_ref.rest_8_), channel_id=1, source_target_pairs={{0,4},{5,1},{4,8},{9,5},{8,12},{13,9},{12,14},{15,13},{14,10},{11,... | collective-permute-start | bytes 798728 | tf_op jit(solution)/shard_map/ppermute | solution.py:271
  55.0 5.4 %collective-permute-start.23 = (bf16[1040,128]{1,0:T(8,128)(2,1)S(1)}, bf16[1040,128]{1,0:T(8,128)(2,1)S(1)}, u32[]{:S(2)}, u32[]{:S(2)}) collective-permute-start(bf16[1040,128]{1,0:T(8,128)(2,1)S(1)} %collective-permute-done.22.buf_ref.rest_8_), channel_id=1, source_target_pairs={{0,1},{1,0},{2,3},{3,2},{4,5},{5,4},{6,7},{7,6},{8,9},{9,8},{10,11... | collective-permute-start | bytes 798728 | tf_op jit(solution)/shard_map/ppermute | solution.py:268
  57.2 6.4 %collective-permute-start.28 = (bf16[1040,128]{1,0:T(8,128)(2,1)S(1)}, bf16[1040,128]{1,0:T(8,128)(2,1)S(1)}, u32[]{:S(2)}, u32[]{:S(2)}) collective-permute-start(bf16[1040,128]{1,0:T(8,128)(2,1)S(1)} %collective-permute-done.24.buf_ref.rest_10_), channel_id=1, source_target_pairs={{0,4},{5,1},{4,8},{9,5},{8,12},{13,9},{12,14},{15,13},{14,10},{11,... | collective-permute-start | bytes 798728 | tf_op jit(solution)/shard_map/ppermute | solution.py:271
  58.5 2.6 %collective-permute-start.25 = (bf16[1040,128]{1,0:T(8,128)(2,1)S(1)}, bf16[1040,128]{1,0:T(8,128)(2,1)S(1)}, u32[]{:S(2)}, u32[]{:S(2)}) collective-permute-start(bf16[1040,128]{1,0:T(8,128)(2,1)S(1)} %collective-permute-done.24.buf_ref.rest_10_), channel_id=1, source_target_pairs={{0,1},{1,0},{2,3},{3,2},{4,5},{5,4},{6,7},{7,6},{8,9},{9,8},{10,11... | collective-permute-start | bytes 798728 | tf_op jit(solution)/shard_map/ppermute | solution.py:268
  60.4 3.2 %collective-permute-start.27 = (bf16[1040,128]{1,0:T(8,128)(2,1)S(1)}, bf16[1040,128]{1,0:T(8,128)(2,1)S(1)}, u32[]{:S(2)}, u32[]{:S(2)}) collective-permute-start(bf16[1040,128]{1,0:T(8,128)(2,1)S(1)} %collective-permute-done.26.buf_ref.rest_12_), channel_id=1, source_target_pairs={{0,1},{1,0},{2,3},{3,2},{4,5},{5,4},{6,7},{7,6},{8,9},{9,8},{10,11... | collective-permute-start | bytes 798728 | tf_op jit(solution)/shard_map/ppermute | solution.py:268
  63.7 1.5 %collective-permute-start.29 = (bf16[1040,128]{1,0:T(8,128)(2,1)S(1)}, bf16[1040,128]{1,0:T(8,128)(2,1)S(1)}, u32[]{:S(2)}, u32[]{:S(2)}) collective-permute-start(bf16[1040,128]{1,0:T(8,128)(2,1)S(1)} %collective-permute-done.28.buf_ref.rest_14_), channel_id=1, source_target_pairs={{0,1},{1,0},{2,3},{3,2},{4,5},{5,4},{6,7},{7,6},{8,9},{9,8},{10,11... | collective-permute-start | bytes 798728 | tf_op jit(solution)/shard_map/ppermute | solution.py:268
  68.1 2.0 %collective-permute-start.30 = (bf16[1040,128]{1,0:T(8,128)(2,1)S(1)}, bf16[1040,128]{1,0:T(8,128)(2,1)S(1)}, u32[]{:S(2)}, u32[]{:S(2)}) collective-permute-start(bf16[1040,128]{1,0:T(8,128)(2,1)S(1)} %get-tuple-element.48.buf_ref.rest_0_), channel_id=1, source_target_pairs={{0,1},{1,0},{2,3},{3,2},{4,5},{5,4},{6,7},{7,6},{8,9},{9,8},{10,11... | collective-permute-start | bytes 798728 | tf_op jit(solution)/shard_map/ppermute | solution.py:268
  68.8 6.4 %collective-permute-start.31 = (bf16[1040,128]{1,0:T(8,128)(2,1)S(1)}, bf16[1040,128]{1,0:T(8,128)(2,1)S(1)}, u32[]{:S(2)}, u32[]{:S(2)}) collective-permute-start(bf16[1040,128]{1,0:T(8,128)(2,1)S(1)} %get-tuple-element.48.buf_ref.rest_0_), channel_id=1, source_target_pairs={{0,4},{5,1},{4,8},{9,5},{8,12},{13,9},{12,14},{15,13},{14,10},{11,... | collective-permute-start | bytes 798728 | tf_op jit(solution)/shard_map/ppermute | solution.py:271
  70.1 8.0 %collective-permute-start.33 = (bf16[1040,128]{1,0:T(8,128)(2,1)S(1)}, bf16[1040,128]{1,0:T(8,128)(2,1)S(1)}, u32[]{:S(2)}, u32[]{:S(2)}) collective-permute-start(bf16[1040,128]{1,0:T(8,128)(2,1)S(1)} %collective-permute-done.30.buf_ref.rest_1_), channel_id=1, source_target_pairs={{0,4},{5,1},{4,8},{9,5},{8,12},{13,9},{12,14},{15,13},{14,10},{11,... | collective-permute-start | bytes 798728 | tf_op jit(solution)/shard_map/ppermute | solution.py:271
  75.2 6.4 %collective-permute-start.35 = (bf16[1040,128]{1,0:T(8,128)(2,1)S(1)}, bf16[1040,128]{1,0:T(8,128)(2,1)S(1)}, u32[]{:S(2)}, u32[]{:S(2)}) collective-permute-start(bf16[1040,128]{1,0:T(8,128)(2,1)S(1)} %collective-permute-done.31.buf_ref.rest_2_), channel_id=1, source_target_pairs={{0,4},{5,1},{4,8},{9,5},{8,12},{13,9},{12,14},{15,13},{14,10},{11,... | collective-permute-start | bytes 798728 | tf_op jit(solution)/shard_map/ppermute | solution.py:271
  76.5 9.4 %collective-permute-start.32 = (bf16[1040,128]{1,0:T(8,128)(2,1)S(1)}, bf16[1040,128]{1,0:T(8,128)(2,1)S(1)}, u32[]{:S(2)}, u32[]{:S(2)}) collective-permute-start(bf16[1040,128]{1,0:T(8,128)(2,1)S(1)} %collective-permute-done.31.buf_ref.rest_2_), channel_id=1, source_target_pairs={{0,1},{1,0},{2,3},{3,2},{4,5},{5,4},{6,7},{7,6},{8,9},{9,8},{10,11... | collective-permute-start | bytes 798728 | tf_op jit(solution)/shard_map/ppermute | solution.py:268
  78.1 6.7 %collective-permute-start.37 = (bf16[1040,128]{1,0:T(8,128)(2,1)S(1)}, bf16[1040,128]{1,0:T(8,128)(2,1)S(1)}, u32[]{:S(2)}, u32[]{:S(2)}) collective-permute-start(bf16[1040,128]{1,0:T(8,128)(2,1)S(1)} %collective-permute-done.33.buf_ref.rest_4_), channel_id=1, source_target_pairs={{0,4},{5,1},{4,8},{9,5},{8,12},{13,9},{12,14},{15,13},{14,10},{11,... | collective-permute-start | bytes 798728 | tf_op jit(solution)/shard_map/ppermute | solution.py:271
  79.4 10.0 %collective-permute-start.34 = (bf16[1040,128]{1,0:T(8,128)(2,1)S(1)}, bf16[1040,128]{1,0:T(8,128)(2,1)S(1)}, u32[]{:S(2)}, u32[]{:S(2)}) collective-permute-start(bf16[1040,128]{1,0:T(8,128)(2,1)S(1)} %collective-permute-done.33.buf_ref.rest_4_), channel_id=1, source_target_pairs={{0,1},{1,0},{2,3},{3,2},{4,5},{5,4},{6,7},{7,6},{8,9},{9,8},{10,11... | collective-permute-start | bytes 798728 | tf_op jit(solution)/shard_map/ppermute | solution.py:268
  81.6 6.4 %collective-permute-start.39 = (bf16[1040,128]{1,0:T(8,128)(2,1)S(1)}, bf16[1040,128]{1,0:T(8,128)(2,1)S(1)}, u32[]{:S(2)}, u32[]{:S(2)}) collective-permute-start(bf16[1040,128]{1,0:T(8,128)(2,1)S(1)} %collective-permute-done.35.buf_ref.rest_6_), channel_id=1, source_target_pairs={{0,4},{5,1},{4,8},{9,5},{8,12},{13,9},{12,14},{15,13},{14,10},{11,... | collective-permute-start | bytes 798728 | tf_op jit(solution)/shard_map/ppermute | solution.py:271
  83.6 6.5 %collective-permute-start.36 = (bf16[1040,128]{1,0:T(8,128)(2,1)S(1)}, bf16[1040,128]{1,0:T(8,128)(2,1)S(1)}, u32[]{:S(2)}, u32[]{:S(2)}) collective-permute-start(bf16[1040,128]{1,0:T(8,128)(2,1)S(1)} %collective-permute-done.35.buf_ref.rest_6_), channel_id=1, source_target_pairs={{0,1},{1,0},{2,3},{3,2},{4,5},{5,4},{6,7},{7,6},{8,9},{9,8},{10,11... | collective-permute-start | bytes 798728 | tf_op jit(solution)/shard_map/ppermute | solution.py:268
  84.7 6.5 %collective-permute-start.41 = (bf16[1040,128]{1,0:T(8,128)(2,1)S(1)}, bf16[1040,128]{1,0:T(8,128)(2,1)S(1)}, u32[]{:S(2)}, u32[]{:S(2)}) collective-permute-start(bf16[1040,128]{1,0:T(8,128)(2,1)S(1)} %collective-permute-done.37.buf_ref.rest_8_), channel_id=1, source_target_pairs={{0,4},{5,1},{4,8},{9,5},{8,12},{13,9},{12,14},{15,13},{14,10},{11,... | collective-permute-start | bytes 798728 | tf_op jit(solution)/shard_map/ppermute | solution.py:271
  85.9 5.3 %collective-permute-start.38 = (bf16[1040,128]{1,0:T(8,128)(2,1)S(1)}, bf16[1040,128]{1,0:T(8,128)(2,1)S(1)}, u32[]{:S(2)}, u32[]{:S(2)}) collective-permute-start(bf16[1040,128]{1,0:T(8,128)(2,1)S(1)} %collective-permute-done.37.buf_ref.rest_8_), channel_id=1, source_target_pairs={{0,1},{1,0},{2,3},{3,2},{4,5},{5,4},{6,7},{7,6},{8,9},{9,8},{10,11... | collective-permute-start | bytes 798728 | tf_op jit(solution)/shard_map/ppermute | solution.py:268
  88.1 6.4 %collective-permute-start.43 = (bf16[1040,128]{1,0:T(8,128)(2,1)S(1)}, bf16[1040,128]{1,0:T(8,128)(2,1)S(1)}, u32[]{:S(2)}, u32[]{:S(2)}) collective-permute-start(bf16[1040,128]{1,0:T(8,128)(2,1)S(1)} %collective-permute-done.39.buf_ref.rest_10_), channel_id=1, source_target_pairs={{0,4},{5,1},{4,8},{9,5},{8,12},{13,9},{12,14},{15,13},{14,10},{11,... | collective-permute-start | bytes 798728 | tf_op jit(solution)/shard_map/ppermute | solution.py:271
  89.3 2.6 %collective-permute-start.40 = (bf16[1040,128]{1,0:T(8,128)(2,1)S(1)}, bf16[1040,128]{1,0:T(8,128)(2,1)S(1)}, u32[]{:S(2)}, u32[]{:S(2)}) collective-permute-start(bf16[1040,128]{1,0:T(8,128)(2,1)S(1)} %collective-permute-done.39.buf_ref.rest_10_), channel_id=1, source_target_pairs={{0,1},{1,0},{2,3},{3,2},{4,5},{5,4},{6,7},{7,6},{8,9},{9,8},{10,11... | collective-permute-start | bytes 798728 | tf_op jit(solution)/shard_map/ppermute | solution.py:268
  91.2 3.3 %collective-permute-start.42 = (bf16[1040,128]{1,0:T(8,128)(2,1)S(1)}, bf16[1040,128]{1,0:T(8,128)(2,1)S(1)}, u32[]{:S(2)}, u32[]{:S(2)}) collective-permute-start(bf16[1040,128]{1,0:T(8,128)(2,1)S(1)} %collective-permute-done.41.buf_ref.rest_12_), channel_id=1, source_target_pairs={{0,1},{1,0},{2,3},{3,2},{4,5},{5,4},{6,7},{7,6},{8,9},{9,8},{10,11... | collective-permute-start | bytes 798728 | tf_op jit(solution)/shard_map/ppermute | solution.py:268
  94.5 1.5 %collective-permute-start.44 = (bf16[1040,128]{1,0:T(8,128)(2,1)S(1)}, bf16[1040,128]{1,0:T(8,128)(2,1)S(1)}, u32[]{:S(2)}, u32[]{:S(2)}) collective-permute-start(bf16[1040,128]{1,0:T(8,128)(2,1)S(1)} %collective-permute-done.43.buf_ref.rest_14_), channel_id=1, source_target_pairs={{0,1},{1,0},{2,3},{3,2},{4,5},{5,4},{6,7},{7,6},{8,9},{9,8},{10,11... | collective-permute-start | bytes 798728 | tf_op jit(solution)/shard_map/ppermute | solution.py:268
  100.5 3.6 %collective-permute-start.46 = (f32[8,128]{1,0:T(8,128)S(1)}, f32[8,128]{1,0:T(8,128)S(1)}, u32[]{:S(2)}, u32[]{:S(2)}) collective-permute-start(f32[8,128]{1,0:T(8,128)S(1)} %add.16), channel_id=1, source_target_pairs={{0,2},{1,3},{2,0},{3,1},{4,6},{5,7},{6,4},{7,5},{8,10},{9,11},{10,... | collective-permute-start | bytes 12296 | tf_op jit(solution)/shard_map/ppermute | solution.py:413
  104.1 3.6 %collective-permute-start.47 = (f32[8,128]{1,0:T(8,128)S(1)}, f32[8,128]{1,0:T(8,128)S(1)}, u32[]{:S(2)}, u32[]{:S(2)}) collective-permute-start(f32[8,128]{1,0:T(8,128)S(1)} %add.17), channel_id=1, source_target_pairs={{0,4},{1,5},{2,6},{3,7},{4,0},{5,1},{6,2},{7,3},{8,12},{9,13},{10,... | collective-permute-start | bytes 12296 | tf_op jit(solution)/shard_map/ppermute | solution.py:413
  107.7 4.6 %collective-permute-start.48 = (f32[8,128]{1,0:T(8,128)S(1)}, f32[8,128]{1,0:T(8,128)S(1)}, u32[]{:S(2)}, u32[]{:S(2)}) collective-permute-start(f32[8,128]{1,0:T(8,128)S(1)} %add.18), channel_id=1, source_target_pairs={{0,8},{1,9},{2,10},{3,11},{4,12},{5,13},{6,14},{7,15},{8,0},{9,1},... | collective-permute-start | bytes 12296 | tf_op jit(solution)/shard_map/ppermute | solution.py:413
  (6 other events, 27.9 us)
where the time goes:
time: 113 us
  starting transfers between devices  40.3 us (36%)
  waiting for transfers between devices  37.6 us (33%)
  Pallas kernels  31.3 us (28%)
  local copies, waits for them, and re-layouts  2.62 us (2%)
    ppermute x21, starting transfers between devices, step_on(): return lax.ppermute(x, 'sector', onward)  31.4 us
    ppermute x21, waiting for transfers between devices, step_on(): return lax.ppermute(x, 'sector', onward)  28.1 us
    pallas_call x48, Pallas kernels, contract(): pl.pallas_call(functools.partial(left_kernel, phase, 10 if phase > peers...  17.7 us
    pallas_call x3, Pallas kernels, apply_operator(): pl.pallas_call(functools.partial(apply_kernel, stage, sizes, slots), out_...  8.73 us
    ppermute x4, waiting for transfers between devices, per_device(): stats = stats + lax.ppermute(stats, 'sector', pairs)  6.46 us
    ppermute x4, starting transfers between devices, per_device(): stats = stats + lax.ppermute(stats, 'sector', pairs)  6.05 us
    pallas_call x1, Pallas kernels, prepare(): pl.pallas_call(functools.partial(prepare_kernel, sizes, phases, peers, us...  4.02 us
    ppermute x24, waiting for transfers between devices, swap_cores(): return lax.ppermute(x, 'sector', sibling)  3.04 us
  transfers between devices with their start and end apart: 49, of which 25 were waited for; matrix products, arithmetic and copies ran while one was open for 1% of the time, Pallas kernels for 19%

commit v1 on v0

--- a/solution.py
+++ b/solution.py
@@ -368,7 +368,7 @@
     def contract(phase, buffer, near, held, *more):
         env_near, right_near, counts, lists, places = near
         return pl.pallas_call(
-            functools.partial(left_kernel, phase, 10 if phase > peers - 3 else 5, sizes),
+            functools.partial(left_kernel, phase, 10 if phase > peers - 5 else 4, sizes),
             out_shape=left_type,
             in_specs=[smem, smem] + [vmem] * (2 + len(held) + len(more)),
             out_specs=vmem,

time: 113 us -> 114 us (level)
  waiting for transfers between devices: 37.6 us -> 32.4 us
  Pallas kernels: 31.3 us -> 34.5 us
  starting transfers between devices: 40.3 us -> 42.5 us
    ppermute x21, waiting for transfers between devices: 28.1 us -> 22.2 us  [step_on(): return lax.ppermute(x, 'sector', onward)]
    pallas_call x48, Pallas kernels: 17.7 us -> 20.9 us  [contract(): pl.pallas_call(functools.partial(left_kernel, phase, 10 if phase > peers...]
    ppermute x24, starting transfers between devices: 2.82 us -> 4.17 us  [swap_cores(): return lax.ppermute(x, 'sector', sibling)]
    ppermute x21, starting transfers between devices: 31.4 us -> 32.6 us  [step_on(): return lax.ppermute(x, 'sector', onward)]
  transfers between devices with their start and end apart: 49 -> 49, of which waited for: 25 -> 23; matrix products, arithmetic and copies ran while one was open for 1% -> 1% of each run, Pallas kernels for 19% -> 22%
where the time goes in v1:
time: 114 us
  starting transfers between devices  42.5 us (37%)
  Pallas kernels  34.5 us (30%)
  waiting for transfers between devices  32.4 us (28%)
  local copies, waits for them, and re-layouts  3.29 us (3%)
    ppermute x21, starting transfers between devices, step_on(): return lax.ppermute(x, 'sector', onward)  32.6 us
    ppermute x21, waiting for transfers between devices, step_on(): return lax.ppermute(x, 'sector', onward)  22.2 us
    pallas_call x48, Pallas kernels, contract(): pl.pallas_call(functools.partial(left_kernel, phase, 10 if phase > peers...  20.9 us
    pallas_call x3, Pallas kernels, apply_operator(): pl.pallas_call(functools.partial(apply_kernel, stage, sizes, slots), out_...  8.74 us
    ppermute x4, waiting for transfers between devices, per_device(): stats = stats + lax.ppermute(stats, 'sector', pairs)  6.8 us
    ppermute x4, starting transfers between devices, per_device(): stats = stats + lax.ppermute(stats, 'sector', pairs)  5.68 us
    ppermute x24, starting transfers between devices, swap_cores(): return lax.ppermute(x, 'sector', sibling)  4.17 us
    pallas_call x1, Pallas kernels, prepare(): pl.pallas_call(functools.partial(prepare_kernel, sizes, phases, peers, us...  4.02 us
  transfers between devices with their start and end apart: 49, of which 23 were waited for; matrix products, arithmetic and copies ran while one was open for 1% of the time, Pallas kernels for 22%

profile of v1, /device:TPU:0, one launch (start us, length us, event | category | flops | bytes accessed | tf_op | source)
XLA Modules:
  0.0 113.9 jit_solution(14309816922359159254)
XLA Ops:
  0.7 0.9 copy-done.3
  2.3 1.2 %collective-permute-done.buf_ref.rest_1_ = bf16[1040,128]{1,0:T(8,128)(2,1)S(1)} collective-permute-done((bf16[1040,128]{1,0:T(8,128)(2,1)S(1)}, bf16[1040,128]{1,0:T(8,128)(2,1)S(1)}, u32[]{:S(2)}, u32[]{:S(2)}) %collective-permute-start) | collective-permute-done | bytes 266272 | tf_op jit(solution)/shard_map/ppermute | solution.py:268
  3.5 2.9 %collective-permute-start.1 = (bf16[1040,128]{1,0:T(8,128)(2,1)S(1)}, bf16[1040,128]{1,0:T(8,128)(2,1)S(1)}, u32[]{:S(2)}, u32[]{:S(2)}) collective-permute-start(bf16[1040,128]{1,0:T(8,128)(2,1)S(1)} %shard_map.59.buf_ref.rest_0_), channel_id=1, source_target_pairs={{0,4},{5,1},{4,8},{9,5},{8,12},{13,9},{12,14},{15,13},{14,10},{11,... | collective-permute-start | bytes 798728 | tf_op jit(solution)/shard_map/ppermute | solution.py:271
  6.6 1.6 %collective-permute-start.3 = (bf16[1040,128]{1,0:T(8,128)(2,1)S(1)}, bf16[1040,128]{1,0:T(8,128)(2,1)S(1)}, u32[]{:S(2)}, u32[]{:S(2)}) collective-permute-start(bf16[1040,128]{1,0:T(8,128)(2,1)S(1)} %collective-permute-done.buf_ref.rest_1_), channel_id=1, source_target_pairs={{0,4},{5,1},{4,8},{9,5},{8,12},{13,9},{12,14},{15,13},{14,10},{11,... | collective-permute-start | bytes 798728 | tf_op jit(solution)/shard_map/ppermute | solution.py:271
  8.2 4.0 %shard_map.60 = (s32[16]{0:T(128)S(4)}, s32[3,1280]{1,0:T(4,128)S(4)}, s32[16]{0:T(128)S(4)}, bf16[40960,128]{1,0:T(8,128)(2,1)S(1)}) custom-call(s32[1]{0:T(128)} %bitcast.1.own_ref, s32[80]{0:T(128)S(1)} %reshape.16.first_ref.second_ref, s32[80]{0:T(128)S(1)} %reshape.16.first_ref.second_ref, bf16[40960,128]{1,0:T(8,128)(2,1)} %bitcast.7), custom_call_target="tpu_custom_call" | custom-call | tf_op jit(solution)/shard_map/pallas_call | solution.py:349
  12.3 1.6 %collective-permute-start.5 = (bf16[1040,128]{1,0:T(8,128)(2,1)S(1)}, bf16[1040,128]{1,0:T(8,128)(2,1)S(1)}, u32[]{:S(2)}, u32[]{:S(2)}) collective-permute-start(bf16[1040,128]{1,0:T(8,128)(2,1)S(1)} %collective-permute-done.1.buf_ref.rest_2_), channel_id=1, source_target_pairs={{0,4},{5,1},{4,8},{9,5},{8,12},{13,9},{12,14},{15,13},{14,10},{11,... | collective-permute-start | bytes 798728 | tf_op jit(solution)/shard_map/ppermute | solution.py:271
  13.9 1.8 %collective-permute-start.7 = (bf16[1040,128]{1,0:T(8,128)(2,1)S(1)}, bf16[1040,128]{1,0:T(8,128)(2,1)S(1)}, u32[]{:S(2)}, u32[]{:S(2)}) collective-permute-start(bf16[1040,128]{1,0:T(8,128)(2,1)S(1)} %collective-permute-done.3.buf_ref.rest_4_), channel_id=1, source_target_pairs={{0,4},{5,1},{4,8},{9,5},{8,12},{13,9},{12,14},{15,13},{14,10},{11,... | collective-permute-start | bytes 798728 | tf_op jit(solution)/shard_map/ppermute | solution.py:271
  15.7 3.1 %collective-permute-done.5.buf_ref.rest_6_ = bf16[1040,128]{1,0:T(8,128)(2,1)S(1)} collective-permute-done((bf16[1040,128]{1,0:T(8,128)(2,1)S(1)}, bf16[1040,128]{1,0:T(8,128)(2,1)S(1)}, u32[]{:S(2)}, u32[]{:S(2)}) %collective-permute-start.5) | collective-permute-done | bytes 266272 | tf_op jit(solution)/shard_map/ppermute | solution.py:271
  18.7 1.6 %collective-permute-start.9 = (bf16[1040,128]{1,0:T(8,128)(2,1)S(1)}, bf16[1040,128]{1,0:T(8,128)(2,1)S(1)}, u32[]{:S(2)}, u32[]{:S(2)}) collective-permute-start(bf16[1040,128]{1,0:T(8,128)(2,1)S(1)} %collective-permute-done.5.buf_ref.rest_6_), channel_id=1, source_target_pairs={{0,4},{5,1},{4,8},{9,5},{8,12},{13,9},{12,14},{15,13},{14,10},{11,... | collective-permute-start | bytes 798728 | tf_op jit(solution)/shard_map/ppermute | solution.py:271
  21.6 1.6 %collective-permute-start.11 = (bf16[1040,128]{1,0:T(8,128)(2,1)S(1)}, bf16[1040,128]{1,0:T(8,128)(2,1)S(1)}, u32[]{:S(2)}, u32[]{:S(2)}) collective-permute-start(bf16[1040,128]{1,0:T(8,128)(2,1)S(1)} %collective-permute-done.7.buf_ref.rest_8_), channel_id=1, source_target_pairs={{0,4},{5,1},{4,8},{9,5},{8,12},{13,9},{12,14},{15,13},{14,10},{11,... | collective-permute-start | bytes 798728 | tf_op jit(solution)/shard_map/ppermute | solution.py:271
  23.2 0.9 shard_map.64.rest_0_
  25.2 1.9 %collective-permute-start.13 = (bf16[1040,128]{1,0:T(8,128)(2,1)S(1)}, bf16[1040,128]{1,0:T(8,128)(2,1)S(1)}, u32[]{:S(2)}, u32[]{:S(2)}) collective-permute-start(bf16[1040,128]{1,0:T(8,128)(2,1)S(1)} %collective-permute-done.9.buf_ref.rest_10_), channel_id=1, source_target_pairs={{0,4},{5,1},{4,8},{9,5},{8,12},{13,9},{12,14},{15,13},{14,10},{11,... | collective-permute-start | bytes 798728 | tf_op jit(solution)/shard_map/ppermute | solution.py:271
  29.9 0.9 shard_map.71.rest_0_
  31.7 1.3 %copy-done.2 = bf16[40,128,128]{2,1,0:T(8,128)(2,1)S(1)} copy-done((bf16[40,128,128]{2,1,0:T(8,128)(2,1)S(1)}, bf16[40,128,128]{2,1,0:T(8,128)(2,1)}, u32[]{:S(2)}) %copy-start.2) | copy-done | bytes 1310744
  33.5 2.9 %shard_map.77 = (f32[1024,128]{1,0:T(8,128)S(1)}, f32[8,128]{1,0:T(8,128)S(1)}, bf16[1040,128]{1,0:T(8,128)(2,1)S(1)}) custom-call(s32[16]{0:T(128)S(4)} %get-tuple-element.34.stat_ref, bf16[5120,128]{1,0:T(8,128)(2,1)S(1)} %bitcast.4, bf16[1024,128]{1,0:T(8,128)(2,1)S(1)} %copy-done.4, bf16[1040,128]{1,0:T(8,128)(2,1)S(1)} %shard_map.59.buf_ref.rest_0_, ...), custom_call_target="tpu_custom_call" | custom-call | flops 2684354560 | bytes 16777216 | tf_op jit(solution)/shard_map/pallas_call | solution.py:390
  36.4 1.6 %collective-permute-start.15 = (bf16[1040,128]{1,0:T(8,128)(2,1)S(1)}, bf16[1040,128]{1,0:T(8,128)(2,1)S(1)}, u32[]{:S(2)}, u32[]{:S(2)}) collective-permute-start(bf16[1040,128]{1,0:T(8,128)(2,1)S(1)} %get-tuple-element.43.buf_ref.rest_0_), channel_id=1, source_target_pairs={{0,1},{1,0},{2,3},{3,2},{4,5},{5,4},{6,7},{7,6},{8,9},{9,8},{10,11... | collective-permute-start | bytes 798728 | tf_op jit(solution)/shard_map/ppermute | solution.py:268
  38.0 1.5 %collective-permute-start.16 = (bf16[1040,128]{1,0:T(8,128)(2,1)S(1)}, bf16[1040,128]{1,0:T(8,128)(2,1)S(1)}, u32[]{:S(2)}, u32[]{:S(2)}) collective-permute-start(bf16[1040,128]{1,0:T(8,128)(2,1)S(1)} %get-tuple-element.43.buf_ref.rest_0_), channel_id=1, source_target_pairs={{0,4},{5,1},{4,8},{9,5},{8,12},{13,9},{12,14},{15,13},{14,10},{11,... | collective-permute-start | bytes 798728 | tf_op jit(solution)/shard_map/ppermute | solution.py:271
  39.5 2.3 %collective-permute-start.18 = (bf16[1040,128]{1,0:T(8,128)(2,1)S(1)}, bf16[1040,128]{1,0:T(8,128)(2,1)S(1)}, u32[]{:S(2)}, u32[]{:S(2)}) collective-permute-start(bf16[1040,128]{1,0:T(8,128)(2,1)S(1)} %collective-permute-done.15.buf_ref.rest_1_), channel_id=1, source_target_pairs={{0,4},{5,1},{4,8},{9,5},{8,12},{13,9},{12,14},{15,13},{14,10},{11,... | collective-permute-start | bytes 798728 | tf_op jit(solution)/shard_map/ppermute | solution.py:271
  41.8 2.6 %collective-permute-done.16.buf_ref.rest_2_ = bf16[1040,128]{1,0:T(8,128)(2,1)S(1)} collective-permute-done((bf16[1040,128]{1,0:T(8,128)(2,1)S(1)}, bf16[1040,128]{1,0:T(8,128)(2,1)S(1)}, u32[]{:S(2)}, u32[]{:S(2)}) %collective-permute-start.16) | collective-permute-done | bytes 266272 | tf_op jit(solution)/shard_map/ppermute | solution.py:271
  44.4 1.5 %collective-permute-start.20 = (bf16[1040,128]{1,0:T(8,128)(2,1)S(1)}, bf16[1040,128]{1,0:T(8,128)(2,1)S(1)}, u32[]{:S(2)}, u32[]{:S(2)}) collective-permute-start(bf16[1040,128]{1,0:T(8,128)(2,1)S(1)} %collective-permute-done.16.buf_ref.rest_2_), channel_id=1, source_target_pairs={{0,4},{5,1},{4,8},{9,5},{8,12},{13,9},{12,14},{15,13},{14,10},{11,... | collective-permute-start | bytes 798728 | tf_op jit(solution)/shard_map/ppermute | solution.py:271
  45.9 1.4 %collective-permute-done.18.buf_ref.rest_4_ = bf16[1040,128]{1,0:T(8,128)(2,1)S(1)} collective-permute-done((bf16[1040,128]{1,0:T(8,128)(2,1)S(1)}, bf16[1040,128]{1,0:T(8,128)(2,1)S(1)}, u32[]{:S(2)}, u32[]{:S(2)}) %collective-permute-start.18) | collective-permute-done | bytes 266272 | tf_op jit(solution)/shard_map/ppermute | solution.py:271
  47.3 1.5 %collective-permute-start.22 = (bf16[1040,128]{1,0:T(8,128)(2,1)S(1)}, bf16[1040,128]{1,0:T(8,128)(2,1)S(1)}, u32[]{:S(2)}, u32[]{:S(2)}) collective-permute-start(bf16[1040,128]{1,0:T(8,128)(2,1)S(1)} %collective-permute-done.18.buf_ref.rest_4_), channel_id=1, source_target_pairs={{0,4},{5,1},{4,8},{9,5},{8,12},{13,9},{12,14},{15,13},{14,10},{11,... | collective-permute-start | bytes 798728 | tf_op jit(solution)/shard_map/ppermute | solution.py:271
  48.8 2.1 %collective-permute-done.20.buf_ref.rest_6_ = bf16[1040,128]{1,0:T(8,128)(2,1)S(1)} collective-permute-done((bf16[1040,128]{1,0:T(8,128)(2,1)S(1)}, bf16[1040,128]{1,0:T(8,128)(2,1)S(1)}, u32[]{:S(2)}, u32[]{:S(2)}) %collective-permute-start.20) | collective-permute-done | bytes 266272 | tf_op jit(solution)/shard_map/ppermute | solution.py:271
  50.8 1.5 %collective-permute-start.24 = (bf16[1040,128]{1,0:T(8,128)(2,1)S(1)}, bf16[1040,128]{1,0:T(8,128)(2,1)S(1)}, u32[]{:S(2)}, u32[]{:S(2)}) collective-permute-start(bf16[1040,128]{1,0:T(8,128)(2,1)S(1)} %collective-permute-done.20.buf_ref.rest_6_), channel_id=1, source_target_pairs={{0,4},{5,1},{4,8},{9,5},{8,12},{13,9},{12,14},{15,13},{14,10},{11,... | collective-permute-start | bytes 798728 | tf_op jit(solution)/shard_map/ppermute | solution.py:271
  53.7 2.6 %collective-permute-start.26 = (bf16[1040,128]{1,0:T(8,128)(2,1)S(1)}, bf16[1040,128]{1,0:T(8,128)(2,1)S(1)}, u32[]{:S(2)}, u32[]{:S(2)}) collective-permute-start(bf16[1040,128]{1,0:T(8,128)(2,1)S(1)} %collective-permute-done.22.buf_ref.rest_8_), channel_id=1, source_target_pairs={{0,4},{5,1},{4,8},{9,5},{8,12},{13,9},{12,14},{15,13},{14,10},{11,... | collective-permute-start | bytes 798728 | tf_op jit(solution)/shard_map/ppermute | solution.py:271
  57.2 0.9 shard_map.82.rest_0_
  60.1 0.9 shard_map.86.rest_0_
  62.5 0.9 shard_map.88.rest_0_
  65.2 1.0 collective-permute-done.29.buf_ref.rest_15_
  66.2 2.9 %shard_map.94 = (f32[1024,128]{1,0:T(8,128)S(1)}, f32[8,128]{1,0:T(8,128)S(1)}, bf16[1040,128]{1,0:T(8,128)(2,1)S(1)}) custom-call(s32[16]{0:T(128)S(4)} %get-tuple-element.34.stat_ref, bf16[5120,128]{1,0:T(8,128)(2,1)S(1)} %bitcast.5, bf16[1024,128]{1,0:T(8,128)(2,1)S(1)} %copy-done.4, bf16[1040,128]{1,0:T(8,128)(2,1)S(1)} %get-tuple-element.43.buf_ref.rest_0_, ...), custom_call_target="tpu_custom_call" | custom-call | flops 2684354560 | bytes 16777216 | tf_op jit(solution)/shard_map/pallas_call | solution.py:390
  70.9 1.7 %collective-permute-start.33 = (bf16[1040,128]{1,0:T(8,128)(2,1)S(1)}, bf16[1040,128]{1,0:T(8,128)(2,1)S(1)}, u32[]{:S(2)}, u32[]{:S(2)}) collective-permute-start(bf16[1040,128]{1,0:T(8,128)(2,1)S(1)} %collective-permute-done.30.buf_ref.rest_1_), channel_id=1, source_target_pairs={{0,4},{5,1},{4,8},{9,5},{8,12},{13,9},{12,14},{15,13},{14,10},{11,... | collective-permute-start | bytes 798728 | tf_op jit(solution)/shard_map/ppermute | solution.py:271
  72.6 3.6 %collective-permute-done.31.buf_ref.rest_2_ = bf16[1040,128]{1,0:T(8,128)(2,1)S(1)} collective-permute-done((bf16[1040,128]{1,0:T(8,128)(2,1)S(1)}, bf16[1040,128]{1,0:T(8,128)(2,1)S(1)}, u32[]{:S(2)}, u32[]{:S(2)}) %collective-permute-start.31) | collective-permute-done | bytes 266272 | tf_op jit(solution)/shard_map/ppermute | solution.py:271
  77.1 2.0 %collective-permute-done.33.buf_ref.rest_4_ = bf16[1040,128]{1,0:T(8,128)(2,1)S(1)} collective-permute-done((bf16[1040,128]{1,0:T(8,128)(2,1)S(1)}, bf16[1040,128]{1,0:T(8,128)(2,1)S(1)}, u32[]{:S(2)}, u32[]{:S(2)}) %collective-permute-start.33) | collective-permute-done | bytes 266272 | tf_op jit(solution)/shard_map/ppermute | solution.py:271
  79.9 2.7 %collective-permute-done.35.buf_ref.rest_6_ = bf16[1040,128]{1,0:T(8,128)(2,1)S(1)} collective-permute-done((bf16[1040,128]{1,0:T(8,128)(2,1)S(1)}, bf16[1040,128]{1,0:T(8,128)(2,1)S(1)}, u32[]{:S(2)}, u32[]{:S(2)}) %collective-permute-start.35) | collective-permute-done | bytes 266272 | tf_op jit(solution)/shard_map/ppermute | solution.py:271
  84.2 1.2 %collective-permute-done.37.buf_ref.rest_8_ = bf16[1040,128]{1,0:T(8,128)(2,1)S(1)} collective-permute-done((bf16[1040,128]{1,0:T(8,128)(2,1)S(1)}, bf16[1040,128]{1,0:T(8,128)(2,1)S(1)}, u32[]{:S(2)}, u32[]{:S(2)}) %collective-permute-start.37) | collective-permute-done | bytes 266272 | tf_op jit(solution)/shard_map/ppermute | solution.py:271
  85.5 1.7 %collective-permute-start.41 = (bf16[1040,128]{1,0:T(8,128)(2,1)S(1)}, bf16[1040,128]{1,0:T(8,128)(2,1)S(1)}, u32[]{:S(2)}, u32[]{:S(2)}) collective-permute-start(bf16[1040,128]{1,0:T(8,128)(2,1)S(1)} %collective-permute-done.37.buf_ref.rest_8_), channel_id=1, source_target_pairs={{0,4},{5,1},{4,8},{9,5},{8,12},{13,9},{12,14},{15,13},{14,10},{11,... | collective-permute-start | bytes 798728 | tf_op jit(solution)/shard_map/ppermute | solution.py:271
  88.0 0.9 shard_map.99.rest_0_
  89.0 1.0 collective-permute-start.43
  90.9 0.9 shard_map.103.rest_0_
  93.3 0.9 shard_map.105.rest_0_
  96.0 1.0 collective-permute-done.44.buf_ref.rest_15_
  97.0 3.0 %shard_map.111 = (f32[1024,128]{1,0:T(8,128)S(1)}, f32[8,128]{1,0:T(8,128)S(1)}, f32[8,128]{1,0:T(8,128)S(1)}) custom-call(s32[16]{0:T(128)S(4)} %get-tuple-element.34.stat_ref, bf16[5120,128]{1,0:T(8,128)(2,1)S(1)} %bitcast.6, bf16[1024,128]{1,0:T(8,128)(2,1)S(1)} %copy-done.4, bf16[1040,128]{1,0:T(8,128)(2,1)S(1)} %get-tuple-element.48.buf_ref.rest_0_, ...), custom_call_target="tpu_custom_call" | custom-call | flops 2684354560 | bytes 16777216 | tf_op jit(solution)/shard_map/pallas_call | solution.py:390
  101.5 1.5 %collective-permute-start.46 = (f32[8,128]{1,0:T(8,128)S(1)}, f32[8,128]{1,0:T(8,128)S(1)}, u32[]{:S(2)}, u32[]{:S(2)}) collective-permute-start(f32[8,128]{1,0:T(8,128)S(1)} %add.16), channel_id=1, source_target_pairs={{0,2},{1,3},{2,0},{3,1},{4,6},{5,7},{6,4},{7,5},{8,10},{9,11},{10,... | collective-permute-start | bytes 12296 | tf_op jit(solution)/shard_map/ppermute | solution.py:413
  103.0 2.1 %collective-permute-done.46 = f32[8,128]{1,0:T(8,128)S(1)} collective-permute-done((f32[8,128]{1,0:T(8,128)S(1)}, f32[8,128]{1,0:T(8,128)S(1)}, u32[]{:S(2)}, u32[]{:S(2)}) %collective-permute-start.46) | collective-permute-done | bytes 4128 | tf_op jit(solution)/shard_map/ppermute | solution.py:413
  105.1 1.2 %collective-permute-start.47 = (f32[8,128]{1,0:T(8,128)S(1)}, f32[8,128]{1,0:T(8,128)S(1)}, u32[]{:S(2)}, u32[]{:S(2)}) collective-permute-start(f32[8,128]{1,0:T(8,128)S(1)} %add.17), channel_id=1, source_target_pairs={{0,4},{1,5},{2,6},{3,7},{4,0},{5,1},{6,2},{7,3},{8,12},{9,13},{10,... | collective-permute-start | bytes 12296 | tf_op jit(solution)/shard_map/ppermute | solution.py:413
  106.3 2.4 %collective-permute-done.47 = f32[8,128]{1,0:T(8,128)S(1)} collective-permute-done((f32[8,128]{1,0:T(8,128)S(1)}, f32[8,128]{1,0:T(8,128)S(1)}, u32[]{:S(2)}, u32[]{:S(2)}) %collective-permute-start.47) | collective-permute-done | bytes 4128 | tf_op jit(solution)/shard_map/ppermute | solution.py:413
  108.7 2.3 %collective-permute-start.48 = (f32[8,128]{1,0:T(8,128)S(1)}, f32[8,128]{1,0:T(8,128)S(1)}, u32[]{:S(2)}, u32[]{:S(2)}) collective-permute-start(f32[8,128]{1,0:T(8,128)S(1)} %add.18), channel_id=1, source_target_pairs={{0,8},{1,9},{2,10},{3,11},{4,12},{5,13},{6,14},{7,15},{8,0},{9,1},... | collective-permute-start | bytes 12296 | tf_op jit(solution)/shard_map/ppermute | solution.py:413
  111.8 1.4 %collective-permute-done.48 = f32[8,128]{1,0:T(8,128)S(1)} collective-permute-done((f32[8,128]{1,0:T(8,128)S(1)}, f32[8,128]{1,0:T(8,128)S(1)}, u32[]{:S(2)}, u32[]{:S(2)}) %collective-permute-start.48) | collective-permute-done | bytes 4128 | tf_op jit(solution)/shard_map/ppermute | solution.py:413
  (122 shorter events, 28.1 us)
Async XLA Ops:
  1.8 1.7 %collective-permute-start = (bf16[1040,128]{1,0:T(8,128)(2,1)S(1)}, bf16[1040,128]{1,0:T(8,128)(2,1)S(1)}, u32[]{:S(2)}, u32[]{:S(2)}) collective-permute-start(bf16[1040,128]{1,0:T(8,128)(2,1)S(1)} %shard_map.59.buf_ref.rest_0_), channel_id=1, source_target_pairs={{0,1},{1,0},{2,3},{3,2},{4,5},{5,4},{6,7},{7,6},{8,9},{9,8},{10,11... | collective-permute-start | bytes 798728 | tf_op jit(solution)/shard_map/ppermute | solution.py:268
  3.5 8.8 %collective-permute-start.1 = (bf16[1040,128]{1,0:T(8,128)(2,1)S(1)}, bf16[1040,128]{1,0:T(8,128)(2,1)S(1)}, u32[]{:S(2)}, u32[]{:S(2)}) collective-permute-start(bf16[1040,128]{1,0:T(8,128)(2,1)S(1)} %shard_map.59.buf_ref.rest_0_), channel_id=1, source_target_pairs={{0,4},{5,1},{4,8},{9,5},{8,12},{13,9},{12,14},{15,13},{14,10},{11,... | collective-permute-start | bytes 798728 | tf_op jit(solution)/shard_map/ppermute | solution.py:271
  6.6 7.3 %collective-permute-start.3 = (bf16[1040,128]{1,0:T(8,128)(2,1)S(1)}, bf16[1040,128]{1,0:T(8,128)(2,1)S(1)}, u32[]{:S(2)}, u32[]{:S(2)}) collective-permute-start(bf16[1040,128]{1,0:T(8,128)(2,1)S(1)} %collective-permute-done.buf_ref.rest_1_), channel_id=1, source_target_pairs={{0,4},{5,1},{4,8},{9,5},{8,12},{13,9},{12,14},{15,13},{14,10},{11,... | collective-permute-start | bytes 798728 | tf_op jit(solution)/shard_map/ppermute | solution.py:271
  12.3 6.5 %collective-permute-start.5 = (bf16[1040,128]{1,0:T(8,128)(2,1)S(1)}, bf16[1040,128]{1,0:T(8,128)(2,1)S(1)}, u32[]{:S(2)}, u32[]{:S(2)}) collective-permute-start(bf16[1040,128]{1,0:T(8,128)(2,1)S(1)} %collective-permute-done.1.buf_ref.rest_2_), channel_id=1, source_target_pairs={{0,4},{5,1},{4,8},{9,5},{8,12},{13,9},{12,14},{15,13},{14,10},{11,... | collective-permute-start | bytes 798728 | tf_op jit(solution)/shard_map/ppermute | solution.py:271
  13.9 9.3 %collective-permute-start.2 = (bf16[1040,128]{1,0:T(8,128)(2,1)S(1)}, bf16[1040,128]{1,0:T(8,128)(2,1)S(1)}, u32[]{:S(2)}, u32[]{:S(2)}) collective-permute-start(bf16[1040,128]{1,0:T(8,128)(2,1)S(1)} %collective-permute-done.1.buf_ref.rest_2_), channel_id=1, source_target_pairs={{0,1},{1,0},{2,3},{3,2},{4,5},{5,4},{6,7},{7,6},{8,9},{9,8},{10,11... | collective-permute-start | bytes 798728 | tf_op jit(solution)/shard_map/ppermute | solution.py:268
  13.9 7.7 %collective-permute-start.7 = (bf16[1040,128]{1,0:T(8,128)(2,1)S(1)}, bf16[1040,128]{1,0:T(8,128)(2,1)S(1)}, u32[]{:S(2)}, u32[]{:S(2)}) collective-permute-start(bf16[1040,128]{1,0:T(8,128)(2,1)S(1)} %collective-permute-done.3.buf_ref.rest_4_), channel_id=1, source_target_pairs={{0,4},{5,1},{4,8},{9,5},{8,12},{13,9},{12,14},{15,13},{14,10},{11,... | collective-permute-start | bytes 798728 | tf_op jit(solution)/shard_map/ppermute | solution.py:271
  15.7 9.5 %collective-permute-start.4 = (bf16[1040,128]{1,0:T(8,128)(2,1)S(1)}, bf16[1040,128]{1,0:T(8,128)(2,1)S(1)}, u32[]{:S(2)}, u32[]{:S(2)}) collective-permute-start(bf16[1040,128]{1,0:T(8,128)(2,1)S(1)} %collective-permute-done.3.buf_ref.rest_4_), channel_id=1, source_target_pairs={{0,1},{1,0},{2,3},{3,2},{4,5},{5,4},{6,7},{7,6},{8,9},{9,8},{10,11... | collective-permute-start | bytes 798728 | tf_op jit(solution)/shard_map/ppermute | solution.py:268
  18.7 6.4 %collective-permute-start.9 = (bf16[1040,128]{1,0:T(8,128)(2,1)S(1)}, bf16[1040,128]{1,0:T(8,128)(2,1)S(1)}, u32[]{:S(2)}, u32[]{:S(2)}) collective-permute-start(bf16[1040,128]{1,0:T(8,128)(2,1)S(1)} %collective-permute-done.5.buf_ref.rest_6_), channel_id=1, source_target_pairs={{0,4},{5,1},{4,8},{9,5},{8,12},{13,9},{12,14},{15,13},{14,10},{11,... | collective-permute-start | bytes 798728 | tf_op jit(solution)/shard_map/ppermute | solution.py:271
  20.9 7.1 %collective-permute-start.6 = (bf16[1040,128]{1,0:T(8,128)(2,1)S(1)}, bf16[1040,128]{1,0:T(8,128)(2,1)S(1)}, u32[]{:S(2)}, u32[]{:S(2)}) collective-permute-start(bf16[1040,128]{1,0:T(8,128)(2,1)S(1)} %collective-permute-done.5.buf_ref.rest_6_), channel_id=1, source_target_pairs={{0,1},{1,0},{2,3},{3,2},{4,5},{5,4},{6,7},{7,6},{8,9},{9,8},{10,11... | collective-permute-start | bytes 798728 | tf_op jit(solution)/shard_map/ppermute | solution.py:268
  21.6 6.4 %collective-permute-start.11 = (bf16[1040,128]{1,0:T(8,128)(2,1)S(1)}, bf16[1040,128]{1,0:T(8,128)(2,1)S(1)}, u32[]{:S(2)}, u32[]{:S(2)}) collective-permute-start(bf16[1040,128]{1,0:T(8,128)(2,1)S(1)} %collective-permute-done.7.buf_ref.rest_8_), channel_id=1, source_target_pairs={{0,4},{5,1},{4,8},{9,5},{8,12},{13,9},{12,14},{15,13},{14,10},{11,... | collective-permute-start | bytes 798728 | tf_op jit(solution)/shard_map/ppermute | solution.py:271
  23.2 5.8 %collective-permute-start.8 = (bf16[1040,128]{1,0:T(8,128)(2,1)S(1)}, bf16[1040,128]{1,0:T(8,128)(2,1)S(1)}, u32[]{:S(2)}, u32[]{:S(2)}) collective-permute-start(bf16[1040,128]{1,0:T(8,128)(2,1)S(1)} %collective-permute-done.7.buf_ref.rest_8_), channel_id=1, source_target_pairs={{0,1},{1,0},{2,3},{3,2},{4,5},{5,4},{6,7},{7,6},{8,9},{9,8},{10,11... | collective-permute-start | bytes 798728 | tf_op jit(solution)/shard_map/ppermute | solution.py:268
  25.2 5.7 %collective-permute-start.10 = (bf16[1040,128]{1,0:T(8,128)(2,1)S(1)}, bf16[1040,128]{1,0:T(8,128)(2,1)S(1)}, u32[]{:S(2)}, u32[]{:S(2)}) collective-permute-start(bf16[1040,128]{1,0:T(8,128)(2,1)S(1)} %collective-permute-done.9.buf_ref.rest_10_), channel_id=1, source_target_pairs={{0,1},{1,0},{2,3},{3,2},{4,5},{5,4},{6,7},{7,6},{8,9},{9,8},{10,11... | collective-permute-start | bytes 798728 | tf_op jit(solution)/shard_map/ppermute | solution.py:268
  25.2 6.5 %collective-permute-start.13 = (bf16[1040,128]{1,0:T(8,128)(2,1)S(1)}, bf16[1040,128]{1,0:T(8,128)(2,1)S(1)}, u32[]{:S(2)}, u32[]{:S(2)}) collective-permute-start(bf16[1040,128]{1,0:T(8,128)(2,1)S(1)} %collective-permute-done.9.buf_ref.rest_10_), channel_id=1, source_target_pairs={{0,4},{5,1},{4,8},{9,5},{8,12},{13,9},{12,14},{15,13},{14,10},{11,... | collective-permute-start | bytes 798728 | tf_op jit(solution)/shard_map/ppermute | solution.py:271
  28.0 3.6 %collective-permute-start.12 = (bf16[1040,128]{1,0:T(8,128)(2,1)S(1)}, bf16[1040,128]{1,0:T(8,128)(2,1)S(1)}, u32[]{:S(2)}, u32[]{:S(2)}) collective-permute-start(bf16[1040,128]{1,0:T(8,128)(2,1)S(1)} %collective-permute-done.11.buf_ref.rest_12_), channel_id=1, source_target_pairs={{0,1},{1,0},{2,3},{3,2},{4,5},{5,4},{6,7},{7,6},{8,9},{9,8},{10,11... | collective-permute-start | bytes 798728 | tf_op jit(solution)/shard_map/ppermute | solution.py:268
  31.6 1.9 %collective-permute-start.14 = (bf16[1040,128]{1,0:T(8,128)(2,1)S(1)}, bf16[1040,128]{1,0:T(8,128)(2,1)S(1)}, u32[]{:S(2)}, u32[]{:S(2)}) collective-permute-start(bf16[1040,128]{1,0:T(8,128)(2,1)S(1)} %collective-permute-done.13.buf_ref.rest_14_), channel_id=1, source_target_pairs={{0,1},{1,0},{2,3},{3,2},{4,5},{5,4},{6,7},{7,6},{8,9},{9,8},{10,11... | collective-permute-start | bytes 798728 | tf_op jit(solution)/shard_map/ppermute | solution.py:268
  36.4 3.1 %collective-permute-start.15 = (bf16[1040,128]{1,0:T(8,128)(2,1)S(1)}, bf16[1040,128]{1,0:T(8,128)(2,1)S(1)}, u32[]{:S(2)}, u32[]{:S(2)}) collective-permute-start(bf16[1040,128]{1,0:T(8,128)(2,1)S(1)} %get-tuple-element.43.buf_ref.rest_0_), channel_id=1, source_target_pairs={{0,1},{1,0},{2,3},{3,2},{4,5},{5,4},{6,7},{7,6},{8,9},{9,8},{10,11... | collective-permute-start | bytes 798728 | tf_op jit(solution)/shard_map/ppermute | solution.py:268
  38.0 6.4 %collective-permute-start.16 = (bf16[1040,128]{1,0:T(8,128)(2,1)S(1)}, bf16[1040,128]{1,0:T(8,128)(2,1)S(1)}, u32[]{:S(2)}, u32[]{:S(2)}) collective-permute-start(bf16[1040,128]{1,0:T(8,128)(2,1)S(1)} %get-tuple-element.43.buf_ref.rest_0_), channel_id=1, source_target_pairs={{0,4},{5,1},{4,8},{9,5},{8,12},{13,9},{12,14},{15,13},{14,10},{11,... | collective-permute-start | bytes 798728 | tf_op jit(solution)/shard_map/ppermute | solution.py:271
  39.5 7.8 %collective-permute-start.18 = (bf16[1040,128]{1,0:T(8,128)(2,1)S(1)}, bf16[1040,128]{1,0:T(8,128)(2,1)S(1)}, u32[]{:S(2)}, u32[]{:S(2)}) collective-permute-start(bf16[1040,128]{1,0:T(8,128)(2,1)S(1)} %collective-permute-done.15.buf_ref.rest_1_), channel_id=1, source_target_pairs={{0,4},{5,1},{4,8},{9,5},{8,12},{13,9},{12,14},{15,13},{14,10},{11,... | collective-permute-start | bytes 798728 | tf_op jit(solution)/shard_map/ppermute | solution.py:271
  44.4 6.4 %collective-permute-start.20 = (bf16[1040,128]{1,0:T(8,128)(2,1)S(1)}, bf16[1040,128]{1,0:T(8,128)(2,1)S(1)}, u32[]{:S(2)}, u32[]{:S(2)}) collective-permute-start(bf16[1040,128]{1,0:T(8,128)(2,1)S(1)} %collective-permute-done.16.buf_ref.rest_2_), channel_id=1, source_target_pairs={{0,4},{5,1},{4,8},{9,5},{8,12},{13,9},{12,14},{15,13},{14,10},{11,... | collective-permute-start | bytes 798728 | tf_op jit(solution)/shard_map/ppermute | solution.py:271
  45.9 10.4 %collective-permute-start.17 = (bf16[1040,128]{1,0:T(8,128)(2,1)S(1)}, bf16[1040,128]{1,0:T(8,128)(2,1)S(1)}, u32[]{:S(2)}, u32[]{:S(2)}) collective-permute-start(bf16[1040,128]{1,0:T(8,128)(2,1)S(1)} %collective-permute-done.16.buf_ref.rest_2_), channel_id=1, source_target_pairs={{0,1},{1,0},{2,3},{3,2},{4,5},{5,4},{6,7},{7,6},{8,9},{9,8},{10,11... | collective-permute-start | bytes 798728 | tf_op jit(solution)/shard_map/ppermute | solution.py:268
  47.3 6.4 %collective-permute-start.22 = (bf16[1040,128]{1,0:T(8,128)(2,1)S(1)}, bf16[1040,128]{1,0:T(8,128)(2,1)S(1)}, u32[]{:S(2)}, u32[]{:S(2)}) collective-permute-start(bf16[1040,128]{1,0:T(8,128)(2,1)S(1)} %collective-permute-done.18.buf_ref.rest_4_), channel_id=1, source_target_pairs={{0,4},{5,1},{4,8},{9,5},{8,12},{13,9},{12,14},{15,13},{14,10},{11,... | collective-permute-start | bytes 798728 | tf_op jit(solution)/shard_map/ppermute | solution.py:271
  48.8 10.3 %collective-permute-start.19 = (bf16[1040,128]{1,0:T(8,128)(2,1)S(1)}, bf16[1040,128]{1,0:T(8,128)(2,1)S(1)}, u32[]{:S(2)}, u32[]{:S(2)}) collective-permute-start(bf16[1040,128]{1,0:T(8,128)(2,1)S(1)} %collective-permute-done.18.buf_ref.rest_4_), channel_id=1, source_target_pairs={{0,1},{1,0},{2,3},{3,2},{4,5},{5,4},{6,7},{7,6},{8,9},{9,8},{10,11... | collective-permute-start | bytes 798728 | tf_op jit(solution)/shard_map/ppermute | solution.py:268
  50.8 7.3 %collective-permute-start.24 = (bf16[1040,128]{1,0:T(8,128)(2,1)S(1)}, bf16[1040,128]{1,0:T(8,128)(2,1)S(1)}, u32[]{:S(2)}, u32[]{:S(2)}) collective-permute-start(bf16[1040,128]{1,0:T(8,128)(2,1)S(1)} %collective-permute-done.20.buf_ref.rest_6_), channel_id=1, source_target_pairs={{0,4},{5,1},{4,8},{9,5},{8,12},{13,9},{12,14},{15,13},{14,10},{11,... | collective-permute-start | bytes 798728 | tf_op jit(solution)/shard_map/ppermute | solution.py:271
  52.9 7.0 %collective-permute-start.21 = (bf16[1040,128]{1,0:T(8,128)(2,1)S(1)}, bf16[1040,128]{1,0:T(8,128)(2,1)S(1)}, u32[]{:S(2)}, u32[]{:S(2)}) collective-permute-start(bf16[1040,128]{1,0:T(8,128)(2,1)S(1)} %collective-permute-done.20.buf_ref.rest_6_), channel_id=1, source_target_pairs={{0,1},{1,0},{2,3},{3,2},{4,5},{5,4},{6,7},{7,6},{8,9},{9,8},{10,11... | collective-permute-start | bytes 798728 | tf_op jit(solution)/shard_map/ppermute | solution.py:268
  53.7 7.4 %collective-permute-start.26 = (bf16[1040,128]{1,0:T(8,128)(2,1)S(1)}, bf16[1040,128]{1,0:T(8,128)(2,1)S(1)}, u32[]{:S(2)}, u32[]{:S(2)}) collective-permute-start(bf16[1040,128]{1,0:T(8,128)(2,1)S(1)} %collective-permute-done.22.buf_ref.rest_8_), channel_id=1, source_target_pairs={{0,4},{5,1},{4,8},{9,5},{8,12},{13,9},{12,14},{15,13},{14,10},{11,... | collective-permute-start | bytes 798728 | tf_op jit(solution)/shard_map/ppermute | solution.py:271
  56.3 5.3 %collective-permute-start.23 = (bf16[1040,128]{1,0:T(8,128)(2,1)S(1)}, bf16[1040,128]{1,0:T(8,128)(2,1)S(1)}, u32[]{:S(2)}, u32[]{:S(2)}) collective-permute-start(bf16[1040,128]{1,0:T(8,128)(2,1)S(1)} %collective-permute-done.22.buf_ref.rest_8_), channel_id=1, source_target_pairs={{0,1},{1,0},{2,3},{3,2},{4,5},{5,4},{6,7},{7,6},{8,9},{9,8},{10,11... | collective-permute-start | bytes 798728 | tf_op jit(solution)/shard_map/ppermute | solution.py:268
  58.1 6.5 %collective-permute-start.28 = (bf16[1040,128]{1,0:T(8,128)(2,1)S(1)}, bf16[1040,128]{1,0:T(8,128)(2,1)S(1)}, u32[]{:S(2)}, u32[]{:S(2)}) collective-permute-start(bf16[1040,128]{1,0:T(8,128)(2,1)S(1)} %collective-permute-done.24.buf_ref.rest_10_), channel_id=1, source_target_pairs={{0,4},{5,1},{4,8},{9,5},{8,12},{13,9},{12,14},{15,13},{14,10},{11,... | collective-permute-start | bytes 798728 | tf_op jit(solution)/shard_map/ppermute | solution.py:271
  59.0 4.4 %collective-permute-start.25 = (bf16[1040,128]{1,0:T(8,128)(2,1)S(1)}, bf16[1040,128]{1,0:T(8,128)(2,1)S(1)}, u32[]{:S(2)}, u32[]{:S(2)}) collective-permute-start(bf16[1040,128]{1,0:T(8,128)(2,1)S(1)} %collective-permute-done.24.buf_ref.rest_10_), channel_id=1, source_target_pairs={{0,1},{1,0},{2,3},{3,2},{4,5},{5,4},{6,7},{7,6},{8,9},{9,8},{10,11... | collective-permute-start | bytes 798728 | tf_op jit(solution)/shard_map/ppermute | solution.py:268
  61.1 3.5 %collective-permute-start.27 = (bf16[1040,128]{1,0:T(8,128)(2,1)S(1)}, bf16[1040,128]{1,0:T(8,128)(2,1)S(1)}, u32[]{:S(2)}, u32[]{:S(2)}) collective-permute-start(bf16[1040,128]{1,0:T(8,128)(2,1)S(1)} %collective-permute-done.26.buf_ref.rest_12_), channel_id=1, source_target_pairs={{0,1},{1,0},{2,3},{3,2},{4,5},{5,4},{6,7},{7,6},{8,9},{9,8},{10,11... | collective-permute-start | bytes 798728 | tf_op jit(solution)/shard_map/ppermute | solution.py:268
  64.6 1.5 %collective-permute-start.29 = (bf16[1040,128]{1,0:T(8,128)(2,1)S(1)}, bf16[1040,128]{1,0:T(8,128)(2,1)S(1)}, u32[]{:S(2)}, u32[]{:S(2)}) collective-permute-start(bf16[1040,128]{1,0:T(8,128)(2,1)S(1)} %collective-permute-done.28.buf_ref.rest_14_), channel_id=1, source_target_pairs={{0,1},{1,0},{2,3},{3,2},{4,5},{5,4},{6,7},{7,6},{8,9},{9,8},{10,11... | collective-permute-start | bytes 798728 | tf_op jit(solution)/shard_map/ppermute | solution.py:268
  69.1 1.9 %collective-permute-start.30 = (bf16[1040,128]{1,0:T(8,128)(2,1)S(1)}, bf16[1040,128]{1,0:T(8,128)(2,1)S(1)}, u32[]{:S(2)}, u32[]{:S(2)}) collective-permute-start(bf16[1040,128]{1,0:T(8,128)(2,1)S(1)} %get-tuple-element.48.buf_ref.rest_0_), channel_id=1, source_target_pairs={{0,1},{1,0},{2,3},{3,2},{4,5},{5,4},{6,7},{7,6},{8,9},{9,8},{10,11... | collective-permute-start | bytes 798728 | tf_op jit(solution)/shard_map/ppermute | solution.py:268
  69.8 6.4 %collective-permute-start.31 = (bf16[1040,128]{1,0:T(8,128)(2,1)S(1)}, bf16[1040,128]{1,0:T(8,128)(2,1)S(1)}, u32[]{:S(2)}, u32[]{:S(2)}) collective-permute-start(bf16[1040,128]{1,0:T(8,128)(2,1)S(1)} %get-tuple-element.48.buf_ref.rest_0_), channel_id=1, source_target_pairs={{0,4},{5,1},{4,8},{9,5},{8,12},{13,9},{12,14},{15,13},{14,10},{11,... | collective-permute-start | bytes 798728 | tf_op jit(solution)/shard_map/ppermute | solution.py:271
  70.9 8.1 %collective-permute-start.33 = (bf16[1040,128]{1,0:T(8,128)(2,1)S(1)}, bf16[1040,128]{1,0:T(8,128)(2,1)S(1)}, u32[]{:S(2)}, u32[]{:S(2)}) collective-permute-start(bf16[1040,128]{1,0:T(8,128)(2,1)S(1)} %collective-permute-done.30.buf_ref.rest_1_), channel_id=1, source_target_pairs={{0,4},{5,1},{4,8},{9,5},{8,12},{13,9},{12,14},{15,13},{14,10},{11,... | collective-permute-start | bytes 798728 | tf_op jit(solution)/shard_map/ppermute | solution.py:271
  76.2 6.4 %collective-permute-start.35 = (bf16[1040,128]{1,0:T(8,128)(2,1)S(1)}, bf16[1040,128]{1,0:T(8,128)(2,1)S(1)}, u32[]{:S(2)}, u32[]{:S(2)}) collective-permute-start(bf16[1040,128]{1,0:T(8,128)(2,1)S(1)} %collective-permute-done.31.buf_ref.rest_2_), channel_id=1, source_target_pairs={{0,4},{5,1},{4,8},{9,5},{8,12},{13,9},{12,14},{15,13},{14,10},{11,... | collective-permute-start | bytes 798728 | tf_op jit(solution)/shard_map/ppermute | solution.py:271
  77.1 10.1 %collective-permute-start.32 = (bf16[1040,128]{1,0:T(8,128)(2,1)S(1)}, bf16[1040,128]{1,0:T(8,128)(2,1)S(1)}, u32[]{:S(2)}, u32[]{:S(2)}) collective-permute-start(bf16[1040,128]{1,0:T(8,128)(2,1)S(1)} %collective-permute-done.31.buf_ref.rest_2_), channel_id=1, source_target_pairs={{0,1},{1,0},{2,3},{3,2},{4,5},{5,4},{6,7},{7,6},{8,9},{9,8},{10,11... | collective-permute-start | bytes 798728 | tf_op jit(solution)/shard_map/ppermute | solution.py:268
  79.0 6.4 %collective-permute-start.37 = (bf16[1040,128]{1,0:T(8,128)(2,1)S(1)}, bf16[1040,128]{1,0:T(8,128)(2,1)S(1)}, u32[]{:S(2)}, u32[]{:S(2)}) collective-permute-start(bf16[1040,128]{1,0:T(8,128)(2,1)S(1)} %collective-permute-done.33.buf_ref.rest_4_), channel_id=1, source_target_pairs={{0,4},{5,1},{4,8},{9,5},{8,12},{13,9},{12,14},{15,13},{14,10},{11,... | collective-permute-start | bytes 798728 | tf_op jit(solution)/shard_map/ppermute | solution.py:271
  79.9 10.1 %collective-permute-start.34 = (bf16[1040,128]{1,0:T(8,128)(2,1)S(1)}, bf16[1040,128]{1,0:T(8,128)(2,1)S(1)}, u32[]{:S(2)}, u32[]{:S(2)}) collective-permute-start(bf16[1040,128]{1,0:T(8,128)(2,1)S(1)} %collective-permute-done.33.buf_ref.rest_4_), channel_id=1, source_target_pairs={{0,1},{1,0},{2,3},{3,2},{4,5},{5,4},{6,7},{7,6},{8,9},{9,8},{10,11... | collective-permute-start | bytes 798728 | tf_op jit(solution)/shard_map/ppermute | solution.py:268
  82.6 6.4 %collective-permute-start.39 = (bf16[1040,128]{1,0:T(8,128)(2,1)S(1)}, bf16[1040,128]{1,0:T(8,128)(2,1)S(1)}, u32[]{:S(2)}, u32[]{:S(2)}) collective-permute-start(bf16[1040,128]{1,0:T(8,128)(2,1)S(1)} %collective-permute-done.35.buf_ref.rest_6_), channel_id=1, source_target_pairs={{0,4},{5,1},{4,8},{9,5},{8,12},{13,9},{12,14},{15,13},{14,10},{11,... | collective-permute-start | bytes 798728 | tf_op jit(solution)/shard_map/ppermute | solution.py:271
  84.1 6.8 %collective-permute-start.36 = (bf16[1040,128]{1,0:T(8,128)(2,1)S(1)}, bf16[1040,128]{1,0:T(8,128)(2,1)S(1)}, u32[]{:S(2)}, u32[]{:S(2)}) collective-permute-start(bf16[1040,128]{1,0:T(8,128)(2,1)S(1)} %collective-permute-done.35.buf_ref.rest_6_), channel_id=1, source_target_pairs={{0,1},{1,0},{2,3},{3,2},{4,5},{5,4},{6,7},{7,6},{8,9},{9,8},{10,11... | collective-permute-start | bytes 798728 | tf_op jit(solution)/shard_map/ppermute | solution.py:268
  85.5 6.4 %collective-permute-start.41 = (bf16[1040,128]{1,0:T(8,128)(2,1)S(1)}, bf16[1040,128]{1,0:T(8,128)(2,1)S(1)}, u32[]{:S(2)}, u32[]{:S(2)}) collective-permute-start(bf16[1040,128]{1,0:T(8,128)(2,1)S(1)} %collective-permute-done.37.buf_ref.rest_8_), channel_id=1, source_target_pairs={{0,4},{5,1},{4,8},{9,5},{8,12},{13,9},{12,14},{15,13},{14,10},{11,... | collective-permute-start | bytes 798728 | tf_op jit(solution)/shard_map/ppermute | solution.py:271
  87.1 5.3 %collective-permute-start.38 = (bf16[1040,128]{1,0:T(8,128)(2,1)S(1)}, bf16[1040,128]{1,0:T(8,128)(2,1)S(1)}, u32[]{:S(2)}, u32[]{:S(2)}) collective-permute-start(bf16[1040,128]{1,0:T(8,128)(2,1)S(1)} %collective-permute-done.37.buf_ref.rest_8_), channel_id=1, source_target_pairs={{0,1},{1,0},{2,3},{3,2},{4,5},{5,4},{6,7},{7,6},{8,9},{9,8},{10,11... | collective-permute-start | bytes 798728 | tf_op jit(solution)/shard_map/ppermute | solution.py:268
  89.0 6.4 %collective-permute-start.43 = (bf16[1040,128]{1,0:T(8,128)(2,1)S(1)}, bf16[1040,128]{1,0:T(8,128)(2,1)S(1)}, u32[]{:S(2)}, u32[]{:S(2)}) collective-permute-start(bf16[1040,128]{1,0:T(8,128)(2,1)S(1)} %collective-permute-done.39.buf_ref.rest_10_), channel_id=1, source_target_pairs={{0,4},{5,1},{4,8},{9,5},{8,12},{13,9},{12,14},{15,13},{14,10},{11,... | collective-permute-start | bytes 798728 | tf_op jit(solution)/shard_map/ppermute | solution.py:271
  90.0 4.2 %collective-permute-start.40 = (bf16[1040,128]{1,0:T(8,128)(2,1)S(1)}, bf16[1040,128]{1,0:T(8,128)(2,1)S(1)}, u32[]{:S(2)}, u32[]{:S(2)}) collective-permute-start(bf16[1040,128]{1,0:T(8,128)(2,1)S(1)} %collective-permute-done.39.buf_ref.rest_10_), channel_id=1, source_target_pairs={{0,1},{1,0},{2,3},{3,2},{4,5},{5,4},{6,7},{7,6},{8,9},{9,8},{10,11... | collective-permute-start | bytes 798728 | tf_op jit(solution)/shard_map/ppermute | solution.py:268
  91.9 3.6 %collective-permute-start.42 = (bf16[1040,128]{1,0:T(8,128)(2,1)S(1)}, bf16[1040,128]{1,0:T(8,128)(2,1)S(1)}, u32[]{:S(2)}, u32[]{:S(2)}) collective-permute-start(bf16[1040,128]{1,0:T(8,128)(2,1)S(1)} %collective-permute-done.41.buf_ref.rest_12_), channel_id=1, source_target_pairs={{0,1},{1,0},{2,3},{3,2},{4,5},{5,4},{6,7},{7,6},{8,9},{9,8},{10,11... | collective-permute-start | bytes 798728 | tf_op jit(solution)/shard_map/ppermute | solution.py:268
  99.9 1.6 %collective-permute-start.45 = (f32[8,128]{1,0:T(8,128)S(1)}, f32[8,128]{1,0:T(8,128)S(1)}, u32[]{:S(2)}, u32[]{:S(2)}) collective-permute-start(f32[8,128]{1,0:T(8,128)S(1)} %get-tuple-element.54), channel_id=1, source_target_pairs={{0,1},{1,0},{2,3},{3,2},{4,5},{5,4},{6,7},{7,6},{8,9},{9,8},{10,11... | collective-permute-start | bytes 12296 | tf_op jit(solution)/shard_map/ppermute | solution.py:413
  101.5 3.6 %collective-permute-start.46 = (f32[8,128]{1,0:T(8,128)S(1)}, f32[8,128]{1,0:T(8,128)S(1)}, u32[]{:S(2)}, u32[]{:S(2)}) collective-permute-start(f32[8,128]{1,0:T(8,128)S(1)} %add.16), channel_id=1, source_target_pairs={{0,2},{1,3},{2,0},{3,1},{4,6},{5,7},{6,4},{7,5},{8,10},{9,11},{10,... | collective-permute-start | bytes 12296 | tf_op jit(solution)/shard_map/ppermute | solution.py:413
  105.1 3.6 %collective-permute-start.47 = (f32[8,128]{1,0:T(8,128)S(1)}, f32[8,128]{1,0:T(8,128)S(1)}, u32[]{:S(2)}, u32[]{:S(2)}) collective-permute-start(f32[8,128]{1,0:T(8,128)S(1)} %add.17), channel_id=1, source_target_pairs={{0,4},{1,5},{2,6},{3,7},{4,0},{5,1},{6,2},{7,3},{8,12},{9,13},{10,... | collective-permute-start | bytes 12296 | tf_op jit(solution)/shard_map/ppermute | solution.py:413
  108.7 4.5 %collective-permute-start.48 = (f32[8,128]{1,0:T(8,128)S(1)}, f32[8,128]{1,0:T(8,128)S(1)}, u32[]{:S(2)}, u32[]{:S(2)}) collective-permute-start(f32[8,128]{1,0:T(8,128)S(1)} %add.18), channel_id=1, source_target_pairs={{0,8},{1,9},{2,10},{3,11},{4,12},{5,13},{6,14},{7,15},{8,0},{9,1},... | collective-permute-start | bytes 12296 | tf_op jit(solution)/shard_map/ppermute | solution.py:413
  (6 other events, 27.8 us)

commit v2 on v1

--- a/solution.py
+++ b/solution.py
@@ -407,11 +407,11 @@
     image_three, coefs_three, stats = apply_operator(
         3, buffers, near, left, [image_one, image_two], [coefs_two]
     )
-    distance = 1
-    while distance < peers:
+    distance = peers // 2
+    while distance:
         pairs = [(i, i ^ distance) for i in range(peers)]
         stats = stats + lax.ppermute(stats, "sector", pairs)
-        distance *= 2
+        distance //= 2
     projected = pl.pallas_call(
         functools.partial(finish_kernel, total),
         out_shape=jax.ShapeDtypeStruct((3, 3), f32),

time: 114 us -> 113 us (level)
  waiting for transfers between devices: 32.4 us -> 34 us
  Pallas kernels: 34.5 us -> 33.3 us
    ppermute x21, waiting for transfers between devices: 22.2 us -> 24.9 us  [step_on(): return lax.ppermute(x, 'sector', onward)]
    ppermute x21, starting transfers between devices: 32.6 us -> 30.3 us  [step_on(): return lax.ppermute(x, 'sector', onward)]
    ppermute x24, starting transfers between devices: 4.17 us -> 5.74 us  [swap_cores(): return lax.ppermute(x, 'sector', sibling)]
    pallas_call x48, Pallas kernels: 20.9 us -> 19.7 us  [contract(): pl.pallas_call(functools.partial(left_kernel, phase, 10 if phase > peers...]
  transfers between devices with their start and end apart: 49 -> 49, of which waited for: 23 -> 21; matrix products, arithmetic and copies ran while one was open for 1% -> 1% of each run, Pallas kernels for 22% -> 21%
where the time goes in v2:
time: 113 us
  starting transfers between devices  41.5 us (37%)
  waiting for transfers between devices  34 us (30%)
  Pallas kernels  33.3 us (29%)
  local copies, waits for them, and re-layouts  3.28 us (3%)
  between operations  1.18 us (1%)
    ppermute x21, starting transfers between devices, step_on(): return lax.ppermute(x, 'sector', onward)  30.3 us
    ppermute x21, waiting for transfers between devices, step_on(): return lax.ppermute(x, 'sector', onward)  24.9 us
    pallas_call x48, Pallas kernels, contract(): pl.pallas_call(functools.partial(left_kernel, phase, 10 if phase > peers...  19.7 us
    pallas_call x3, Pallas kernels, apply_operator(): pl.pallas_call(functools.partial(apply_kernel, stage, sizes, slots), out_...  8.74 us
    ppermute x4, waiting for transfers between devices, per_device(): stats = stats + lax.ppermute(stats, 'sector', pairs)  6.7 us
    ppermute x24, starting transfers between devices, swap_cores(): return lax.ppermute(x, 'sector', sibling)  5.74 us
    ppermute x4, starting transfers between devices, per_device(): stats = stats + lax.ppermute(stats, 'sector', pairs)  5.46 us
    pallas_call x1, Pallas kernels, prepare(): pl.pallas_call(functools.partial(prepare_kernel, sizes, phases, peers, us...  4.02 us
  transfers between devices with their start and end apart: 49, of which 21 were waited for; matrix products, arithmetic and copies ran while one was open for 1% of the time, Pallas kernels for 21%

profile of v2, /device:TPU:0, one launch (start us, length us, event | category | flops | bytes accessed | tf_op | source)
XLA Modules:
  0.0 113.2 jit_solution(186859187571167961)
XLA Ops:
  0.7 0.9 copy-done.3
  2.3 1.2 %collective-permute-done.buf_ref.rest_1_ = bf16[1040,128]{1,0:T(8,128)(2,1)S(1)} collective-permute-done((bf16[1040,128]{1,0:T(8,128)(2,1)S(1)}, bf16[1040,128]{1,0:T(8,128)(2,1)S(1)}, u32[]{:S(2)}, u32[]{:S(2)}) %collective-permute-start) | collective-permute-done | bytes 266272 | tf_op jit(solution)/shard_map/ppermute | solution.py:268
  3.5 2.9 %collective-permute-start.1 = (bf16[1040,128]{1,0:T(8,128)(2,1)S(1)}, bf16[1040,128]{1,0:T(8,128)(2,1)S(1)}, u32[]{:S(2)}, u32[]{:S(2)}) collective-permute-start(bf16[1040,128]{1,0:T(8,128)(2,1)S(1)} %shard_map.59.buf_ref.rest_0_), channel_id=1, source_target_pairs={{0,4},{5,1},{4,8},{9,5},{8,12},{13,9},{12,14},{15,13},{14,10},{11,... | collective-permute-start | bytes 798728 | tf_op jit(solution)/shard_map/ppermute | solution.py:271
  6.6 1.6 %collective-permute-start.3 = (bf16[1040,128]{1,0:T(8,128)(2,1)S(1)}, bf16[1040,128]{1,0:T(8,128)(2,1)S(1)}, u32[]{:S(2)}, u32[]{:S(2)}) collective-permute-start(bf16[1040,128]{1,0:T(8,128)(2,1)S(1)} %collective-permute-done.buf_ref.rest_1_), channel_id=1, source_target_pairs={{0,4},{5,1},{4,8},{9,5},{8,12},{13,9},{12,14},{15,13},{14,10},{11,... | collective-permute-start | bytes 798728 | tf_op jit(solution)/shard_map/ppermute | solution.py:271
  8.2 4.0 %shard_map.60 = (s32[16]{0:T(128)S(4)}, s32[3,1280]{1,0:T(4,128)S(4)}, s32[16]{0:T(128)S(4)}, bf16[40960,128]{1,0:T(8,128)(2,1)S(1)}) custom-call(s32[1]{0:T(128)} %bitcast.1.own_ref, s32[80]{0:T(128)S(1)} %reshape.16.first_ref.second_ref, s32[80]{0:T(128)S(1)} %reshape.16.first_ref.second_ref, bf16[40960,128]{1,0:T(8,128)(2,1)} %bitcast.7), custom_call_target="tpu_custom_call" | custom-call | tf_op jit(solution)/shard_map/pallas_call | solution.py:349
  12.3 1.6 %collective-permute-start.5 = (bf16[1040,128]{1,0:T(8,128)(2,1)S(1)}, bf16[1040,128]{1,0:T(8,128)(2,1)S(1)}, u32[]{:S(2)}, u32[]{:S(2)}) collective-permute-start(bf16[1040,128]{1,0:T(8,128)(2,1)S(1)} %collective-permute-done.1.buf_ref.rest_2_), channel_id=1, source_target_pairs={{0,4},{5,1},{4,8},{9,5},{8,12},{13,9},{12,14},{15,13},{14,10},{11,... | collective-permute-start | bytes 798728 | tf_op jit(solution)/shard_map/ppermute | solution.py:271
  13.9 1.8 %collective-permute-start.7 = (bf16[1040,128]{1,0:T(8,128)(2,1)S(1)}, bf16[1040,128]{1,0:T(8,128)(2,1)S(1)}, u32[]{:S(2)}, u32[]{:S(2)}) collective-permute-start(bf16[1040,128]{1,0:T(8,128)(2,1)S(1)} %collective-permute-done.3.buf_ref.rest_4_), channel_id=1, source_target_pairs={{0,4},{5,1},{4,8},{9,5},{8,12},{13,9},{12,14},{15,13},{14,10},{11,... | collective-permute-start | bytes 798728 | tf_op jit(solution)/shard_map/ppermute | solution.py:271
  15.7 3.1 %collective-permute-done.5.buf_ref.rest_6_ = bf16[1040,128]{1,0:T(8,128)(2,1)S(1)} collective-permute-done((bf16[1040,128]{1,0:T(8,128)(2,1)S(1)}, bf16[1040,128]{1,0:T(8,128)(2,1)S(1)}, u32[]{:S(2)}, u32[]{:S(2)}) %collective-permute-start.5) | collective-permute-done | bytes 266272 | tf_op jit(solution)/shard_map/ppermute | solution.py:271
  18.7 1.6 %collective-permute-start.9 = (bf16[1040,128]{1,0:T(8,128)(2,1)S(1)}, bf16[1040,128]{1,0:T(8,128)(2,1)S(1)}, u32[]{:S(2)}, u32[]{:S(2)}) collective-permute-start(bf16[1040,128]{1,0:T(8,128)(2,1)S(1)} %collective-permute-done.5.buf_ref.rest_6_), channel_id=1, source_target_pairs={{0,4},{5,1},{4,8},{9,5},{8,12},{13,9},{12,14},{15,13},{14,10},{11,... | collective-permute-start | bytes 798728 | tf_op jit(solution)/shard_map/ppermute | solution.py:271
  21.6 1.6 %collective-permute-start.11 = (bf16[1040,128]{1,0:T(8,128)(2,1)S(1)}, bf16[1040,128]{1,0:T(8,128)(2,1)S(1)}, u32[]{:S(2)}, u32[]{:S(2)}) collective-permute-start(bf16[1040,128]{1,0:T(8,128)(2,1)S(1)} %collective-permute-done.7.buf_ref.rest_8_), channel_id=1, source_target_pairs={{0,4},{5,1},{4,8},{9,5},{8,12},{13,9},{12,14},{15,13},{14,10},{11,... | collective-permute-start | bytes 798728 | tf_op jit(solution)/shard_map/ppermute | solution.py:271
  24.2 0.9 shard_map.65.rest_0_
  25.6 1.2 %collective-permute-start.13 = (bf16[1040,128]{1,0:T(8,128)(2,1)S(1)}, bf16[1040,128]{1,0:T(8,128)(2,1)S(1)}, u32[]{:S(2)}, u32[]{:S(2)}) collective-permute-start(bf16[1040,128]{1,0:T(8,128)(2,1)S(1)} %collective-permute-done.9.buf_ref.rest_10_), channel_id=1, source_target_pairs={{0,4},{5,1},{4,8},{9,5},{8,12},{13,9},{12,14},{15,13},{14,10},{11,... | collective-permute-start | bytes 798728 | tf_op jit(solution)/shard_map/ppermute | solution.py:271
  28.4 0.9 shard_map.71.rest_0_
  29.3 0.9 shard_map.72.rest_0_
  30.2 2.0 %collective-permute-done.13.buf_ref.rest_14_ = bf16[1040,128]{1,0:T(8,128)(2,1)S(1)} collective-permute-done((bf16[1040,128]{1,0:T(8,128)(2,1)S(1)}, bf16[1040,128]{1,0:T(8,128)(2,1)S(1)}, u32[]{:S(2)}, u32[]{:S(2)}) %collective-permute-start.13) | collective-permute-done | bytes 266272 | tf_op jit(solution)/shard_map/ppermute | solution.py:271
  32.9 1.3 %copy-done.2 = bf16[40,128,128]{2,1,0:T(8,128)(2,1)S(1)} copy-done((bf16[40,128,128]{2,1,0:T(8,128)(2,1)S(1)}, bf16[40,128,128]{2,1,0:T(8,128)(2,1)}, u32[]{:S(2)}) %copy-start.2) | copy-done | bytes 1310744
  34.7 2.9 %shard_map.77 = (f32[1024,128]{1,0:T(8,128)S(1)}, f32[8,128]{1,0:T(8,128)S(1)}, bf16[1040,128]{1,0:T(8,128)(2,1)S(1)}) custom-call(s32[16]{0:T(128)S(4)} %get-tuple-element.34.stat_ref, bf16[5120,128]{1,0:T(8,128)(2,1)S(1)} %bitcast.4, bf16[1024,128]{1,0:T(8,128)(2,1)S(1)} %copy-done.4, bf16[1040,128]{1,0:T(8,128)(2,1)S(1)} %shard_map.59.buf_ref.rest_0_, ...), custom_call_target="tpu_custom_call" | custom-call | flops 2684354560 | bytes 16777216 | tf_op jit(solution)/shard_map/pallas_call | solution.py:390
  39.3 1.6 %collective-permute-start.18 = (bf16[1040,128]{1,0:T(8,128)(2,1)S(1)}, bf16[1040,128]{1,0:T(8,128)(2,1)S(1)}, u32[]{:S(2)}, u32[]{:S(2)}) collective-permute-start(bf16[1040,128]{1,0:T(8,128)(2,1)S(1)} %collective-permute-done.15.buf_ref.rest_1_), channel_id=1, source_target_pairs={{0,4},{5,1},{4,8},{9,5},{8,12},{13,9},{12,14},{15,13},{14,10},{11,... | collective-permute-start | bytes 798728 | tf_op jit(solution)/shard_map/ppermute | solution.py:271
  40.8 3.7 %collective-permute-done.16.buf_ref.rest_2_ = bf16[1040,128]{1,0:T(8,128)(2,1)S(1)} collective-permute-done((bf16[1040,128]{1,0:T(8,128)(2,1)S(1)}, bf16[1040,128]{1,0:T(8,128)(2,1)S(1)}, u32[]{:S(2)}, u32[]{:S(2)}) %collective-permute-start.16) | collective-permute-done | bytes 266272 | tf_op jit(solution)/shard_map/ppermute | solution.py:271
  45.4 1.9 %collective-permute-done.18.buf_ref.rest_4_ = bf16[1040,128]{1,0:T(8,128)(2,1)S(1)} collective-permute-done((bf16[1040,128]{1,0:T(8,128)(2,1)S(1)}, bf16[1040,128]{1,0:T(8,128)(2,1)S(1)}, u32[]{:S(2)}, u32[]{:S(2)}) %collective-permute-start.18) | collective-permute-done | bytes 266272 | tf_op jit(solution)/shard_map/ppermute | solution.py:271
  48.3 2.6 %collective-permute-done.20.buf_ref.rest_6_ = bf16[1040,128]{1,0:T(8,128)(2,1)S(1)} collective-permute-done((bf16[1040,128]{1,0:T(8,128)(2,1)S(1)}, bf16[1040,128]{1,0:T(8,128)(2,1)S(1)}, u32[]{:S(2)}, u32[]{:S(2)}) %collective-permute-start.20) | collective-permute-done | bytes 266272 | tf_op jit(solution)/shard_map/ppermute | solution.py:271
  52.4 0.9 shard_map.80.rest_0_
  55.7 1.6 %collective-permute-done.24.buf_ref.rest_10_ = bf16[1040,128]{1,0:T(8,128)(2,1)S(1)} collective-permute-done((bf16[1040,128]{1,0:T(8,128)(2,1)S(1)}, bf16[1040,128]{1,0:T(8,128)(2,1)S(1)}, u32[]{:S(2)}, u32[]{:S(2)}) %collective-permute-start.24) | collective-permute-done | bytes 266272 | tf_op jit(solution)/shard_map/ppermute | solution.py:271
  57.3 1.8 %collective-permute-start.28 = (bf16[1040,128]{1,0:T(8,128)(2,1)S(1)}, bf16[1040,128]{1,0:T(8,128)(2,1)S(1)}, u32[]{:S(2)}, u32[]{:S(2)}) collective-permute-start(bf16[1040,128]{1,0:T(8,128)(2,1)S(1)} %collective-permute-done.24.buf_ref.rest_10_), channel_id=1, source_target_pairs={{0,4},{5,1},{4,8},{9,5},{8,12},{13,9},{12,14},{15,13},{14,10},{11,... | collective-permute-start | bytes 798728 | tf_op jit(solution)/shard_map/ppermute | solution.py:271
  60.6 1.5 %collective-permute-start.27 = (bf16[1040,128]{1,0:T(8,128)(2,1)S(1)}, bf16[1040,128]{1,0:T(8,128)(2,1)S(1)}, u32[]{:S(2)}, u32[]{:S(2)}) collective-permute-start(bf16[1040,128]{1,0:T(8,128)(2,1)S(1)} %collective-permute-done.26.buf_ref.rest_12_), channel_id=1, source_target_pairs={{0,1},{1,0},{2,3},{3,2},{4,5},{5,4},{6,7},{7,6},{8,9},{9,8},{10,11... | collective-permute-start | bytes 798728 | tf_op jit(solution)/shard_map/ppermute | solution.py:268
  63.0 0.9 shard_map.89.rest_0_
  65.6 2.9 %shard_map.94 = (f32[1024,128]{1,0:T(8,128)S(1)}, f32[8,128]{1,0:T(8,128)S(1)}, bf16[1040,128]{1,0:T(8,128)(2,1)S(1)}) custom-call(s32[16]{0:T(128)S(4)} %get-tuple-element.34.stat_ref, bf16[5120,128]{1,0:T(8,128)(2,1)S(1)} %bitcast.5, bf16[1024,128]{1,0:T(8,128)(2,1)S(1)} %copy-done.4, bf16[1040,128]{1,0:T(8,128)(2,1)S(1)} %get-tuple-element.43.buf_ref.rest_0_, ...), custom_call_target="tpu_custom_call" | custom-call | flops 2684354560 | bytes 16777216 | tf_op jit(solution)/shard_map/pallas_call | solution.py:390
  68.7 1.6 %collective-permute-start.31 = (bf16[1040,128]{1,0:T(8,128)(2,1)S(1)}, bf16[1040,128]{1,0:T(8,128)(2,1)S(1)}, u32[]{:S(2)}, u32[]{:S(2)}) collective-permute-start(bf16[1040,128]{1,0:T(8,128)(2,1)S(1)} %get-tuple-element.48.buf_ref.rest_0_), channel_id=1, source_target_pairs={{0,4},{5,1},{4,8},{9,5},{8,12},{13,9},{12,14},{15,13},{14,10},{11,... | collective-permute-start | bytes 798728 | tf_op jit(solution)/shard_map/ppermute | solution.py:271
  70.3 1.5 %collective-permute-start.33 = (bf16[1040,128]{1,0:T(8,128)(2,1)S(1)}, bf16[1040,128]{1,0:T(8,128)(2,1)S(1)}, u32[]{:S(2)}, u32[]{:S(2)}) collective-permute-start(bf16[1040,128]{1,0:T(8,128)(2,1)S(1)} %collective-permute-done.30.buf_ref.rest_1_), channel_id=1, source_target_pairs={{0,4},{5,1},{4,8},{9,5},{8,12},{13,9},{12,14},{15,13},{14,10},{11,... | collective-permute-start | bytes 798728 | tf_op jit(solution)/shard_map/ppermute | solution.py:271
  71.7 3.6 %collective-permute-done.31.buf_ref.rest_2_ = bf16[1040,128]{1,0:T(8,128)(2,1)S(1)} collective-permute-done((bf16[1040,128]{1,0:T(8,128)(2,1)S(1)}, bf16[1040,128]{1,0:T(8,128)(2,1)S(1)}, u32[]{:S(2)}, u32[]{:S(2)}) %collective-permute-start.31) | collective-permute-done | bytes 266272 | tf_op jit(solution)/shard_map/ppermute | solution.py:271
  75.3 1.4 %collective-permute-start.35 = (bf16[1040,128]{1,0:T(8,128)(2,1)S(1)}, bf16[1040,128]{1,0:T(8,128)(2,1)S(1)}, u32[]{:S(2)}, u32[]{:S(2)}) collective-permute-start(bf16[1040,128]{1,0:T(8,128)(2,1)S(1)} %collective-permute-done.31.buf_ref.rest_2_), channel_id=1, source_target_pairs={{0,4},{5,1},{4,8},{9,5},{8,12},{13,9},{12,14},{15,13},{14,10},{11,... | collective-permute-start | bytes 798728 | tf_op jit(solution)/shard_map/ppermute | solution.py:271
  76.7 1.5 %collective-permute-done.33.buf_ref.rest_4_ = bf16[1040,128]{1,0:T(8,128)(2,1)S(1)} collective-permute-done((bf16[1040,128]{1,0:T(8,128)(2,1)S(1)}, bf16[1040,128]{1,0:T(8,128)(2,1)S(1)}, u32[]{:S(2)}, u32[]{:S(2)}) %collective-permute-start.33) | collective-permute-done | bytes 266272 | tf_op jit(solution)/shard_map/ppermute | solution.py:271
  78.2 1.4 %collective-permute-start.37 = (bf16[1040,128]{1,0:T(8,128)(2,1)S(1)}, bf16[1040,128]{1,0:T(8,128)(2,1)S(1)}, u32[]{:S(2)}, u32[]{:S(2)}) collective-permute-start(bf16[1040,128]{1,0:T(8,128)(2,1)S(1)} %collective-permute-done.33.buf_ref.rest_4_), channel_id=1, source_target_pairs={{0,4},{5,1},{4,8},{9,5},{8,12},{13,9},{12,14},{15,13},{14,10},{11,... | collective-permute-start | bytes 798728 | tf_op jit(solution)/shard_map/ppermute | solution.py:271
  79.5 2.2 %collective-permute-done.35.buf_ref.rest_6_ = bf16[1040,128]{1,0:T(8,128)(2,1)S(1)} collective-permute-done((bf16[1040,128]{1,0:T(8,128)(2,1)S(1)}, bf16[1040,128]{1,0:T(8,128)(2,1)S(1)}, u32[]{:S(2)}, u32[]{:S(2)}) %collective-permute-start.35) | collective-permute-done | bytes 266272 | tf_op jit(solution)/shard_map/ppermute | solution.py:271
  81.7 1.4 %collective-permute-start.39 = (bf16[1040,128]{1,0:T(8,128)(2,1)S(1)}, bf16[1040,128]{1,0:T(8,128)(2,1)S(1)}, u32[]{:S(2)}, u32[]{:S(2)}) collective-permute-start(bf16[1040,128]{1,0:T(8,128)(2,1)S(1)} %collective-permute-done.35.buf_ref.rest_6_), channel_id=1, source_target_pairs={{0,4},{5,1},{4,8},{9,5},{8,12},{13,9},{12,14},{15,13},{14,10},{11,... | collective-permute-start | bytes 798728 | tf_op jit(solution)/shard_map/ppermute | solution.py:271
  83.8 0.9 shard_map.97.rest_0_
  84.7 1.2 %collective-permute-start.41 = (bf16[1040,128]{1,0:T(8,128)(2,1)S(1)}, bf16[1040,128]{1,0:T(8,128)(2,1)S(1)}, u32[]{:S(2)}, u32[]{:S(2)}) collective-permute-start(bf16[1040,128]{1,0:T(8,128)(2,1)S(1)} %collective-permute-done.37.buf_ref.rest_8_), channel_id=1, source_target_pairs={{0,4},{5,1},{4,8},{9,5},{8,12},{13,9},{12,14},{15,13},{14,10},{11,... | collective-permute-start | bytes 798728 | tf_op jit(solution)/shard_map/ppermute | solution.py:271
  86.8 1.3 %collective-permute-done.39.buf_ref.rest_10_ = bf16[1040,128]{1,0:T(8,128)(2,1)S(1)} collective-permute-done((bf16[1040,128]{1,0:T(8,128)(2,1)S(1)}, bf16[1040,128]{1,0:T(8,128)(2,1)S(1)}, u32[]{:S(2)}, u32[]{:S(2)}) %collective-permute-start.39) | collective-permute-done | bytes 266272 | tf_op jit(solution)/shard_map/ppermute | solution.py:271
  88.1 2.3 %collective-permute-start.43 = (bf16[1040,128]{1,0:T(8,128)(2,1)S(1)}, bf16[1040,128]{1,0:T(8,128)(2,1)S(1)}, u32[]{:S(2)}, u32[]{:S(2)}) collective-permute-start(bf16[1040,128]{1,0:T(8,128)(2,1)S(1)} %collective-permute-done.39.buf_ref.rest_10_), channel_id=1, source_target_pairs={{0,4},{5,1},{4,8},{9,5},{8,12},{13,9},{12,14},{15,13},{14,10},{11,... | collective-permute-start | bytes 798728 | tf_op jit(solution)/shard_map/ppermute | solution.py:271
  91.7 1.5 %collective-permute-start.42 = (bf16[1040,128]{1,0:T(8,128)(2,1)S(1)}, bf16[1040,128]{1,0:T(8,128)(2,1)S(1)}, u32[]{:S(2)}, u32[]{:S(2)}) collective-permute-start(bf16[1040,128]{1,0:T(8,128)(2,1)S(1)} %collective-permute-done.41.buf_ref.rest_12_), channel_id=1, source_target_pairs={{0,1},{1,0},{2,3},{3,2},{4,5},{5,4},{6,7},{7,6},{8,9},{9,8},{10,11... | collective-permute-start | bytes 798728 | tf_op jit(solution)/shard_map/ppermute | solution.py:268
  94.1 0.9 shard_map.106.rest_0_
  96.6 3.0 %shard_map.111 = (f32[1024,128]{1,0:T(8,128)S(1)}, f32[8,128]{1,0:T(8,128)S(1)}, f32[8,128]{1,0:T(8,128)S(1)}) custom-call(s32[16]{0:T(128)S(4)} %get-tuple-element.34.stat_ref, bf16[5120,128]{1,0:T(8,128)(2,1)S(1)} %bitcast.6, bf16[1024,128]{1,0:T(8,128)(2,1)S(1)} %copy-done.4, bf16[1040,128]{1,0:T(8,128)(2,1)S(1)} %get-tuple-element.48.buf_ref.rest_0_, ...), custom_call_target="tpu_custom_call" | custom-call | flops 2684354560 | bytes 16777216 | tf_op jit(solution)/shard_map/pallas_call | solution.py:390
  99.6 2.2 %collective-permute-start.45 = (f32[8,128]{1,0:T(8,128)S(1)}, f32[8,128]{1,0:T(8,128)S(1)}, u32[]{:S(2)}, u32[]{:S(2)}) collective-permute-start(f32[8,128]{1,0:T(8,128)S(1)} %get-tuple-element.54), channel_id=1, source_target_pairs={{0,8},{1,9},{2,10},{3,11},{4,12},{5,13},{6,14},{7,15},{8,0},{9,1},... | collective-permute-start | bytes 12296 | tf_op jit(solution)/shard_map/ppermute | solution.py:413
  101.8 2.4 %collective-permute-done.45 = f32[8,128]{1,0:T(8,128)S(1)} collective-permute-done((f32[8,128]{1,0:T(8,128)S(1)}, f32[8,128]{1,0:T(8,128)S(1)}, u32[]{:S(2)}, u32[]{:S(2)}) %collective-permute-start.45) | collective-permute-done | bytes 4128 | tf_op jit(solution)/shard_map/ppermute | solution.py:413
  104.2 1.7 %collective-permute-start.46 = (f32[8,128]{1,0:T(8,128)S(1)}, f32[8,128]{1,0:T(8,128)S(1)}, u32[]{:S(2)}, u32[]{:S(2)}) collective-permute-start(f32[8,128]{1,0:T(8,128)S(1)} %add.16), channel_id=1, source_target_pairs={{0,4},{1,5},{2,6},{3,7},{4,0},{5,1},{6,2},{7,3},{8,12},{9,13},{10,... | collective-permute-start | bytes 12296 | tf_op jit(solution)/shard_map/ppermute | solution.py:413
  105.9 1.9 %collective-permute-done.46 = f32[8,128]{1,0:T(8,128)S(1)} collective-permute-done((f32[8,128]{1,0:T(8,128)S(1)}, f32[8,128]{1,0:T(8,128)S(1)}, u32[]{:S(2)}, u32[]{:S(2)}) %collective-permute-start.46) | collective-permute-done | bytes 4128 | tf_op jit(solution)/shard_map/ppermute | solution.py:413
  107.8 1.5 %collective-permute-start.47 = (f32[8,128]{1,0:T(8,128)S(1)}, f32[8,128]{1,0:T(8,128)S(1)}, u32[]{:S(2)}, u32[]{:S(2)}) collective-permute-start(f32[8,128]{1,0:T(8,128)S(1)} %add.17), channel_id=1, source_target_pairs={{0,2},{1,3},{2,0},{3,1},{4,6},{5,7},{6,4},{7,5},{8,10},{9,11},{10,... | collective-permute-start | bytes 12296 | tf_op jit(solution)/shard_map/ppermute | solution.py:413
  109.3 2.1 %collective-permute-done.47 = f32[8,128]{1,0:T(8,128)S(1)} collective-permute-done((f32[8,128]{1,0:T(8,128)S(1)}, f32[8,128]{1,0:T(8,128)S(1)}, u32[]{:S(2)}, u32[]{:S(2)}) %collective-permute-start.47) | collective-permute-done | bytes 4128 | tf_op jit(solution)/shard_map/ppermute | solution.py:413
  (122 shorter events, 25.0 us)
Async XLA Ops:
  1.8 1.7 %collective-permute-start = (bf16[1040,128]{1,0:T(8,128)(2,1)S(1)}, bf16[1040,128]{1,0:T(8,128)(2,1)S(1)}, u32[]{:S(2)}, u32[]{:S(2)}) collective-permute-start(bf16[1040,128]{1,0:T(8,128)(2,1)S(1)} %shard_map.59.buf_ref.rest_0_), channel_id=1, source_target_pairs={{0,1},{1,0},{2,3},{3,2},{4,5},{5,4},{6,7},{7,6},{8,9},{9,8},{10,11... | collective-permute-start | bytes 798728 | tf_op jit(solution)/shard_map/ppermute | solution.py:268
  3.5 8.8 %collective-permute-start.1 = (bf16[1040,128]{1,0:T(8,128)(2,1)S(1)}, bf16[1040,128]{1,0:T(8,128)(2,1)S(1)}, u32[]{:S(2)}, u32[]{:S(2)}) collective-permute-start(bf16[1040,128]{1,0:T(8,128)(2,1)S(1)} %shard_map.59.buf_ref.rest_0_), channel_id=1, source_target_pairs={{0,4},{5,1},{4,8},{9,5},{8,12},{13,9},{12,14},{15,13},{14,10},{11,... | collective-permute-start | bytes 798728 | tf_op jit(solution)/shard_map/ppermute | solution.py:271
  6.6 7.3 %collective-permute-start.3 = (bf16[1040,128]{1,0:T(8,128)(2,1)S(1)}, bf16[1040,128]{1,0:T(8,128)(2,1)S(1)}, u32[]{:S(2)}, u32[]{:S(2)}) collective-permute-start(bf16[1040,128]{1,0:T(8,128)(2,1)S(1)} %collective-permute-done.buf_ref.rest_1_), channel_id=1, source_target_pairs={{0,4},{5,1},{4,8},{9,5},{8,12},{13,9},{12,14},{15,13},{14,10},{11,... | collective-permute-start | bytes 798728 | tf_op jit(solution)/shard_map/ppermute | solution.py:271
  12.3 6.5 %collective-permute-start.5 = (bf16[1040,128]{1,0:T(8,128)(2,1)S(1)}, bf16[1040,128]{1,0:T(8,128)(2,1)S(1)}, u32[]{:S(2)}, u32[]{:S(2)}) collective-permute-start(bf16[1040,128]{1,0:T(8,128)(2,1)S(1)} %collective-permute-done.1.buf_ref.rest_2_), channel_id=1, source_target_pairs={{0,4},{5,1},{4,8},{9,5},{8,12},{13,9},{12,14},{15,13},{14,10},{11,... | collective-permute-start | bytes 798728 | tf_op jit(solution)/shard_map/ppermute | solution.py:271
  13.9 10.2 %collective-permute-start.2 = (bf16[1040,128]{1,0:T(8,128)(2,1)S(1)}, bf16[1040,128]{1,0:T(8,128)(2,1)S(1)}, u32[]{:S(2)}, u32[]{:S(2)}) collective-permute-start(bf16[1040,128]{1,0:T(8,128)(2,1)S(1)} %collective-permute-done.1.buf_ref.rest_2_), channel_id=1, source_target_pairs={{0,1},{1,0},{2,3},{3,2},{4,5},{5,4},{6,7},{7,6},{8,9},{9,8},{10,11... | collective-permute-start | bytes 798728 | tf_op jit(solution)/shard_map/ppermute | solution.py:268
  13.9 7.7 %collective-permute-start.7 = (bf16[1040,128]{1,0:T(8,128)(2,1)S(1)}, bf16[1040,128]{1,0:T(8,128)(2,1)S(1)}, u32[]{:S(2)}, u32[]{:S(2)}) collective-permute-start(bf16[1040,128]{1,0:T(8,128)(2,1)S(1)} %collective-permute-done.3.buf_ref.rest_4_), channel_id=1, source_target_pairs={{0,4},{5,1},{4,8},{9,5},{8,12},{13,9},{12,14},{15,13},{14,10},{11,... | collective-permute-start | bytes 798728 | tf_op jit(solution)/shard_map/ppermute | solution.py:271
  15.7 9.9 %collective-permute-start.4 = (bf16[1040,128]{1,0:T(8,128)(2,1)S(1)}, bf16[1040,128]{1,0:T(8,128)(2,1)S(1)}, u32[]{:S(2)}, u32[]{:S(2)}) collective-permute-start(bf16[1040,128]{1,0:T(8,128)(2,1)S(1)} %collective-permute-done.3.buf_ref.rest_4_), channel_id=1, source_target_pairs={{0,1},{1,0},{2,3},{3,2},{4,5},{5,4},{6,7},{7,6},{8,9},{9,8},{10,11... | collective-permute-start | bytes 798728 | tf_op jit(solution)/shard_map/ppermute | solution.py:268
  18.7 6.4 %collective-permute-start.9 = (bf16[1040,128]{1,0:T(8,128)(2,1)S(1)}, bf16[1040,128]{1,0:T(8,128)(2,1)S(1)}, u32[]{:S(2)}, u32[]{:S(2)}) collective-permute-start(bf16[1040,128]{1,0:T(8,128)(2,1)S(1)} %collective-permute-done.5.buf_ref.rest_6_), channel_id=1, source_target_pairs={{0,4},{5,1},{4,8},{9,5},{8,12},{13,9},{12,14},{15,13},{14,10},{11,... | collective-permute-start | bytes 798728 | tf_op jit(solution)/shard_map/ppermute | solution.py:271
  20.9 7.1 %collective-permute-start.6 = (bf16[1040,128]{1,0:T(8,128)(2,1)S(1)}, bf16[1040,128]{1,0:T(8,128)(2,1)S(1)}, u32[]{:S(2)}, u32[]{:S(2)}) collective-permute-start(bf16[1040,128]{1,0:T(8,128)(2,1)S(1)} %collective-permute-done.5.buf_ref.rest_6_), channel_id=1, source_target_pairs={{0,1},{1,0},{2,3},{3,2},{4,5},{5,4},{6,7},{7,6},{8,9},{9,8},{10,11... | collective-permute-start | bytes 798728 | tf_op jit(solution)/shard_map/ppermute | solution.py:268
  21.6 6.4 %collective-permute-start.11 = (bf16[1040,128]{1,0:T(8,128)(2,1)S(1)}, bf16[1040,128]{1,0:T(8,128)(2,1)S(1)}, u32[]{:S(2)}, u32[]{:S(2)}) collective-permute-start(bf16[1040,128]{1,0:T(8,128)(2,1)S(1)} %collective-permute-done.7.buf_ref.rest_8_), channel_id=1, source_target_pairs={{0,4},{5,1},{4,8},{9,5},{8,12},{13,9},{12,14},{15,13},{14,10},{11,... | collective-permute-start | bytes 798728 | tf_op jit(solution)/shard_map/ppermute | solution.py:271
  24.1 4.3 %collective-permute-start.8 = (bf16[1040,128]{1,0:T(8,128)(2,1)S(1)}, bf16[1040,128]{1,0:T(8,128)(2,1)S(1)}, u32[]{:S(2)}, u32[]{:S(2)}) collective-permute-start(bf16[1040,128]{1,0:T(8,128)(2,1)S(1)} %collective-permute-done.7.buf_ref.rest_8_), channel_id=1, source_target_pairs={{0,1},{1,0},{2,3},{3,2},{4,5},{5,4},{6,7},{7,6},{8,9},{9,8},{10,11... | collective-permute-start | bytes 798728 | tf_op jit(solution)/shard_map/ppermute | solution.py:268
  25.2 4.1 %collective-permute-start.10 = (bf16[1040,128]{1,0:T(8,128)(2,1)S(1)}, bf16[1040,128]{1,0:T(8,128)(2,1)S(1)}, u32[]{:S(2)}, u32[]{:S(2)}) collective-permute-start(bf16[1040,128]{1,0:T(8,128)(2,1)S(1)} %collective-permute-done.9.buf_ref.rest_10_), channel_id=1, source_target_pairs={{0,1},{1,0},{2,3},{3,2},{4,5},{5,4},{6,7},{7,6},{8,9},{9,8},{10,11... | collective-permute-start | bytes 798728 | tf_op jit(solution)/shard_map/ppermute | solution.py:268
  25.6 6.6 %collective-permute-start.13 = (bf16[1040,128]{1,0:T(8,128)(2,1)S(1)}, bf16[1040,128]{1,0:T(8,128)(2,1)S(1)}, u32[]{:S(2)}, u32[]{:S(2)}) collective-permute-start(bf16[1040,128]{1,0:T(8,128)(2,1)S(1)} %collective-permute-done.9.buf_ref.rest_10_), channel_id=1, source_target_pairs={{0,4},{5,1},{4,8},{9,5},{8,12},{13,9},{12,14},{15,13},{14,10},{11,... | collective-permute-start | bytes 798728 | tf_op jit(solution)/shard_map/ppermute | solution.py:271
  28.0 4.8 %collective-permute-start.12 = (bf16[1040,128]{1,0:T(8,128)(2,1)S(1)}, bf16[1040,128]{1,0:T(8,128)(2,1)S(1)}, u32[]{:S(2)}, u32[]{:S(2)}) collective-permute-start(bf16[1040,128]{1,0:T(8,128)(2,1)S(1)} %collective-permute-done.11.buf_ref.rest_12_), channel_id=1, source_target_pairs={{0,1},{1,0},{2,3},{3,2},{4,5},{5,4},{6,7},{7,6},{8,9},{9,8},{10,11... | collective-permute-start | bytes 798728 | tf_op jit(solution)/shard_map/ppermute | solution.py:268
  32.2 2.4 %collective-permute-start.14 = (bf16[1040,128]{1,0:T(8,128)(2,1)S(1)}, bf16[1040,128]{1,0:T(8,128)(2,1)S(1)}, u32[]{:S(2)}, u32[]{:S(2)}) collective-permute-start(bf16[1040,128]{1,0:T(8,128)(2,1)S(1)} %collective-permute-done.13.buf_ref.rest_14_), channel_id=1, source_target_pairs={{0,1},{1,0},{2,3},{3,2},{4,5},{5,4},{6,7},{7,6},{8,9},{9,8},{10,11... | collective-permute-start | bytes 798728 | tf_op jit(solution)/shard_map/ppermute | solution.py:268
  37.6 1.7 %collective-permute-start.15 = (bf16[1040,128]{1,0:T(8,128)(2,1)S(1)}, bf16[1040,128]{1,0:T(8,128)(2,1)S(1)}, u32[]{:S(2)}, u32[]{:S(2)}) collective-permute-start(bf16[1040,128]{1,0:T(8,128)(2,1)S(1)} %get-tuple-element.43.buf_ref.rest_0_), channel_id=1, source_target_pairs={{0,1},{1,0},{2,3},{3,2},{4,5},{5,4},{6,7},{7,6},{8,9},{9,8},{10,11... | collective-permute-start | bytes 798728 | tf_op jit(solution)/shard_map/ppermute | solution.py:268
  38.1 6.4 %collective-permute-start.16 = (bf16[1040,128]{1,0:T(8,128)(2,1)S(1)}, bf16[1040,128]{1,0:T(8,128)(2,1)S(1)}, u32[]{:S(2)}, u32[]{:S(2)}) collective-permute-start(bf16[1040,128]{1,0:T(8,128)(2,1)S(1)} %get-tuple-element.43.buf_ref.rest_0_), channel_id=1, source_target_pairs={{0,4},{5,1},{4,8},{9,5},{8,12},{13,9},{12,14},{15,13},{14,10},{11,... | collective-permute-start | bytes 798728 | tf_op jit(solution)/shard_map/ppermute | solution.py:271
  39.3 8.1 %collective-permute-start.18 = (bf16[1040,128]{1,0:T(8,128)(2,1)S(1)}, bf16[1040,128]{1,0:T(8,128)(2,1)S(1)}, u32[]{:S(2)}, u32[]{:S(2)}) collective-permute-start(bf16[1040,128]{1,0:T(8,128)(2,1)S(1)} %collective-permute-done.15.buf_ref.rest_1_), channel_id=1, source_target_pairs={{0,4},{5,1},{4,8},{9,5},{8,12},{13,9},{12,14},{15,13},{14,10},{11,... | collective-permute-start | bytes 798728 | tf_op jit(solution)/shard_map/ppermute | solution.py:271
  44.5 6.4 %collective-permute-start.20 = (bf16[1040,128]{1,0:T(8,128)(2,1)S(1)}, bf16[1040,128]{1,0:T(8,128)(2,1)S(1)}, u32[]{:S(2)}, u32[]{:S(2)}) collective-permute-start(bf16[1040,128]{1,0:T(8,128)(2,1)S(1)} %collective-permute-done.16.buf_ref.rest_2_), channel_id=1, source_target_pairs={{0,4},{5,1},{4,8},{9,5},{8,12},{13,9},{12,14},{15,13},{14,10},{11,... | collective-permute-start | bytes 798728 | tf_op jit(solution)/shard_map/ppermute | solution.py:271
  45.3 9.3 %collective-permute-start.17 = (bf16[1040,128]{1,0:T(8,128)(2,1)S(1)}, bf16[1040,128]{1,0:T(8,128)(2,1)S(1)}, u32[]{:S(2)}, u32[]{:S(2)}) collective-permute-start(bf16[1040,128]{1,0:T(8,128)(2,1)S(1)} %collective-permute-done.16.buf_ref.rest_2_), channel_id=1, source_target_pairs={{0,1},{1,0},{2,3},{3,2},{4,5},{5,4},{6,7},{7,6},{8,9},{9,8},{10,11... | collective-permute-start | bytes 798728 | tf_op jit(solution)/shard_map/ppermute | solution.py:268
  47.4 6.4 %collective-permute-start.22 = (bf16[1040,128]{1,0:T(8,128)(2,1)S(1)}, bf16[1040,128]{1,0:T(8,128)(2,1)S(1)}, u32[]{:S(2)}, u32[]{:S(2)}) collective-permute-start(bf16[1040,128]{1,0:T(8,128)(2,1)S(1)} %collective-permute-done.18.buf_ref.rest_4_), channel_id=1, source_target_pairs={{0,4},{5,1},{4,8},{9,5},{8,12},{13,9},{12,14},{15,13},{14,10},{11,... | collective-permute-start | bytes 798728 | tf_op jit(solution)/shard_map/ppermute | solution.py:271
  48.2 11.0 %collective-permute-start.19 = (bf16[1040,128]{1,0:T(8,128)(2,1)S(1)}, bf16[1040,128]{1,0:T(8,128)(2,1)S(1)}, u32[]{:S(2)}, u32[]{:S(2)}) collective-permute-start(bf16[1040,128]{1,0:T(8,128)(2,1)S(1)} %collective-permute-done.18.buf_ref.rest_4_), channel_id=1, source_target_pairs={{0,1},{1,0},{2,3},{3,2},{4,5},{5,4},{6,7},{7,6},{8,9},{9,8},{10,11... | collective-permute-start | bytes 798728 | tf_op jit(solution)/shard_map/ppermute | solution.py:268
  50.9 6.4 %collective-permute-start.24 = (bf16[1040,128]{1,0:T(8,128)(2,1)S(1)}, bf16[1040,128]{1,0:T(8,128)(2,1)S(1)}, u32[]{:S(2)}, u32[]{:S(2)}) collective-permute-start(bf16[1040,128]{1,0:T(8,128)(2,1)S(1)} %collective-permute-done.20.buf_ref.rest_6_), channel_id=1, source_target_pairs={{0,4},{5,1},{4,8},{9,5},{8,12},{13,9},{12,14},{15,13},{14,10},{11,... | collective-permute-start | bytes 798728 | tf_op jit(solution)/shard_map/ppermute | solution.py:271
  52.3 7.8 %collective-permute-start.21 = (bf16[1040,128]{1,0:T(8,128)(2,1)S(1)}, bf16[1040,128]{1,0:T(8,128)(2,1)S(1)}, u32[]{:S(2)}, u32[]{:S(2)}) collective-permute-start(bf16[1040,128]{1,0:T(8,128)(2,1)S(1)} %collective-permute-done.20.buf_ref.rest_6_), channel_id=1, source_target_pairs={{0,1},{1,0},{2,3},{3,2},{4,5},{5,4},{6,7},{7,6},{8,9},{9,8},{10,11... | collective-permute-start | bytes 798728 | tf_op jit(solution)/shard_map/ppermute | solution.py:268
  53.8 6.8 %collective-permute-start.26 = (bf16[1040,128]{1,0:T(8,128)(2,1)S(1)}, bf16[1040,128]{1,0:T(8,128)(2,1)S(1)}, u32[]{:S(2)}, u32[]{:S(2)}) collective-permute-start(bf16[1040,128]{1,0:T(8,128)(2,1)S(1)} %collective-permute-done.22.buf_ref.rest_8_), channel_id=1, source_target_pairs={{0,4},{5,1},{4,8},{9,5},{8,12},{13,9},{12,14},{15,13},{14,10},{11,... | collective-permute-start | bytes 798728 | tf_op jit(solution)/shard_map/ppermute | solution.py:271
  54.6 7.5 %collective-permute-start.23 = (bf16[1040,128]{1,0:T(8,128)(2,1)S(1)}, bf16[1040,128]{1,0:T(8,128)(2,1)S(1)}, u32[]{:S(2)}, u32[]{:S(2)}) collective-permute-start(bf16[1040,128]{1,0:T(8,128)(2,1)S(1)} %collective-permute-done.22.buf_ref.rest_8_), channel_id=1, source_target_pairs={{0,1},{1,0},{2,3},{3,2},{4,5},{5,4},{6,7},{7,6},{8,9},{9,8},{10,11... | collective-permute-start | bytes 798728 | tf_op jit(solution)/shard_map/ppermute | solution.py:268
  57.3 6.6 %collective-permute-start.28 = (bf16[1040,128]{1,0:T(8,128)(2,1)S(1)}, bf16[1040,128]{1,0:T(8,128)(2,1)S(1)}, u32[]{:S(2)}, u32[]{:S(2)}) collective-permute-start(bf16[1040,128]{1,0:T(8,128)(2,1)S(1)} %collective-permute-done.24.buf_ref.rest_10_), channel_id=1, source_target_pairs={{0,4},{5,1},{4,8},{9,5},{8,12},{13,9},{12,14},{15,13},{14,10},{11,... | collective-permute-start | bytes 798728 | tf_op jit(solution)/shard_map/ppermute | solution.py:271
  59.2 3.8 %collective-permute-start.25 = (bf16[1040,128]{1,0:T(8,128)(2,1)S(1)}, bf16[1040,128]{1,0:T(8,128)(2,1)S(1)}, u32[]{:S(2)}, u32[]{:S(2)}) collective-permute-start(bf16[1040,128]{1,0:T(8,128)(2,1)S(1)} %collective-permute-done.24.buf_ref.rest_10_), channel_id=1, source_target_pairs={{0,1},{1,0},{2,3},{3,2},{4,5},{5,4},{6,7},{7,6},{8,9},{9,8},{10,11... | collective-permute-start | bytes 798728 | tf_op jit(solution)/shard_map/ppermute | solution.py:268
  60.6 4.0 %collective-permute-start.27 = (bf16[1040,128]{1,0:T(8,128)(2,1)S(1)}, bf16[1040,128]{1,0:T(8,128)(2,1)S(1)}, u32[]{:S(2)}, u32[]{:S(2)}) collective-permute-start(bf16[1040,128]{1,0:T(8,128)(2,1)S(1)} %collective-permute-done.26.buf_ref.rest_12_), channel_id=1, source_target_pairs={{0,1},{1,0},{2,3},{3,2},{4,5},{5,4},{6,7},{7,6},{8,9},{9,8},{10,11... | collective-permute-start | bytes 798728 | tf_op jit(solution)/shard_map/ppermute | solution.py:268
  64.0 1.6 %collective-permute-start.29 = (bf16[1040,128]{1,0:T(8,128)(2,1)S(1)}, bf16[1040,128]{1,0:T(8,128)(2,1)S(1)}, u32[]{:S(2)}, u32[]{:S(2)}) collective-permute-start(bf16[1040,128]{1,0:T(8,128)(2,1)S(1)} %collective-permute-done.28.buf_ref.rest_14_), channel_id=1, source_target_pairs={{0,1},{1,0},{2,3},{3,2},{4,5},{5,4},{6,7},{7,6},{8,9},{9,8},{10,11... | collective-permute-start | bytes 798728 | tf_op jit(solution)/shard_map/ppermute | solution.py:268
  68.5 1.8 %collective-permute-start.30 = (bf16[1040,128]{1,0:T(8,128)(2,1)S(1)}, bf16[1040,128]{1,0:T(8,128)(2,1)S(1)}, u32[]{:S(2)}, u32[]{:S(2)}) collective-permute-start(bf16[1040,128]{1,0:T(8,128)(2,1)S(1)} %get-tuple-element.48.buf_ref.rest_0_), channel_id=1, source_target_pairs={{0,1},{1,0},{2,3},{3,2},{4,5},{5,4},{6,7},{7,6},{8,9},{9,8},{10,11... | collective-permute-start | bytes 798728 | tf_op jit(solution)/shard_map/ppermute | solution.py:268
  68.7 6.6 %collective-permute-start.31 = (bf16[1040,128]{1,0:T(8,128)(2,1)S(1)}, bf16[1040,128]{1,0:T(8,128)(2,1)S(1)}, u32[]{:S(2)}, u32[]{:S(2)}) collective-permute-start(bf16[1040,128]{1,0:T(8,128)(2,1)S(1)} %get-tuple-element.48.buf_ref.rest_0_), channel_id=1, source_target_pairs={{0,4},{5,1},{4,8},{9,5},{8,12},{13,9},{12,14},{15,13},{14,10},{11,... | collective-permute-start | bytes 798728 | tf_op jit(solution)/shard_map/ppermute | solution.py:271
  70.3 7.9 %collective-permute-start.33 = (bf16[1040,128]{1,0:T(8,128)(2,1)S(1)}, bf16[1040,128]{1,0:T(8,128)(2,1)S(1)}, u32[]{:S(2)}, u32[]{:S(2)}) collective-permute-start(bf16[1040,128]{1,0:T(8,128)(2,1)S(1)} %collective-permute-done.30.buf_ref.rest_1_), channel_id=1, source_target_pairs={{0,4},{5,1},{4,8},{9,5},{8,12},{13,9},{12,14},{15,13},{14,10},{11,... | collective-permute-start | bytes 798728 | tf_op jit(solution)/shard_map/ppermute | solution.py:271
  75.3 6.4 %collective-permute-start.35 = (bf16[1040,128]{1,0:T(8,128)(2,1)S(1)}, bf16[1040,128]{1,0:T(8,128)(2,1)S(1)}, u32[]{:S(2)}, u32[]{:S(2)}) collective-permute-start(bf16[1040,128]{1,0:T(8,128)(2,1)S(1)} %collective-permute-done.31.buf_ref.rest_2_), channel_id=1, source_target_pairs={{0,4},{5,1},{4,8},{9,5},{8,12},{13,9},{12,14},{15,13},{14,10},{11,... | collective-permute-start | bytes 798728 | tf_op jit(solution)/shard_map/ppermute | solution.py:271
  76.7 9.3 %collective-permute-start.32 = (bf16[1040,128]{1,0:T(8,128)(2,1)S(1)}, bf16[1040,128]{1,0:T(8,128)(2,1)S(1)}, u32[]{:S(2)}, u32[]{:S(2)}) collective-permute-start(bf16[1040,128]{1,0:T(8,128)(2,1)S(1)} %collective-permute-done.31.buf_ref.rest_2_), channel_id=1, source_target_pairs={{0,1},{1,0},{2,3},{3,2},{4,5},{5,4},{6,7},{7,6},{8,9},{9,8},{10,11... | collective-permute-start | bytes 798728 | tf_op jit(solution)/shard_map/ppermute | solution.py:268
  78.2 6.6 %collective-permute-start.37 = (bf16[1040,128]{1,0:T(8,128)(2,1)S(1)}, bf16[1040,128]{1,0:T(8,128)(2,1)S(1)}, u32[]{:S(2)}, u32[]{:S(2)}) collective-permute-start(bf16[1040,128]{1,0:T(8,128)(2,1)S(1)} %collective-permute-done.33.buf_ref.rest_4_), channel_id=1, source_target_pairs={{0,4},{5,1},{4,8},{9,5},{8,12},{13,9},{12,14},{15,13},{14,10},{11,... | collective-permute-start | bytes 798728 | tf_op jit(solution)/shard_map/ppermute | solution.py:271
  79.5 10.9 %collective-permute-start.34 = (bf16[1040,128]{1,0:T(8,128)(2,1)S(1)}, bf16[1040,128]{1,0:T(8,128)(2,1)S(1)}, u32[]{:S(2)}, u32[]{:S(2)}) collective-permute-start(bf16[1040,128]{1,0:T(8,128)(2,1)S(1)} %collective-permute-done.33.buf_ref.rest_4_), channel_id=1, source_target_pairs={{0,1},{1,0},{2,3},{3,2},{4,5},{5,4},{6,7},{7,6},{8,9},{9,8},{10,11... | collective-permute-start | bytes 798728 | tf_op jit(solution)/shard_map/ppermute | solution.py:268
  81.7 6.4 %collective-permute-start.39 = (bf16[1040,128]{1,0:T(8,128)(2,1)S(1)}, bf16[1040,128]{1,0:T(8,128)(2,1)S(1)}, u32[]{:S(2)}, u32[]{:S(2)}) collective-permute-start(bf16[1040,128]{1,0:T(8,128)(2,1)S(1)} %collective-permute-done.35.buf_ref.rest_6_), channel_id=1, source_target_pairs={{0,4},{5,1},{4,8},{9,5},{8,12},{13,9},{12,14},{15,13},{14,10},{11,... | collective-permute-start | bytes 798728 | tf_op jit(solution)/shard_map/ppermute | solution.py:271
  83.7 7.6 %collective-permute-start.36 = (bf16[1040,128]{1,0:T(8,128)(2,1)S(1)}, bf16[1040,128]{1,0:T(8,128)(2,1)S(1)}, u32[]{:S(2)}, u32[]{:S(2)}) collective-permute-start(bf16[1040,128]{1,0:T(8,128)(2,1)S(1)} %collective-permute-done.35.buf_ref.rest_6_), channel_id=1, source_target_pairs={{0,1},{1,0},{2,3},{3,2},{4,5},{5,4},{6,7},{7,6},{8,9},{9,8},{10,11... | collective-permute-start | bytes 798728 | tf_op jit(solution)/shard_map/ppermute | solution.py:268
  84.7 7.0 %collective-permute-start.41 = (bf16[1040,128]{1,0:T(8,128)(2,1)S(1)}, bf16[1040,128]{1,0:T(8,128)(2,1)S(1)}, u32[]{:S(2)}, u32[]{:S(2)}) collective-permute-start(bf16[1040,128]{1,0:T(8,128)(2,1)S(1)} %collective-permute-done.37.buf_ref.rest_8_), channel_id=1, source_target_pairs={{0,4},{5,1},{4,8},{9,5},{8,12},{13,9},{12,14},{15,13},{14,10},{11,... | collective-permute-start | bytes 798728 | tf_op jit(solution)/shard_map/ppermute | solution.py:271
  85.9 7.2 %collective-permute-start.38 = (bf16[1040,128]{1,0:T(8,128)(2,1)S(1)}, bf16[1040,128]{1,0:T(8,128)(2,1)S(1)}, u32[]{:S(2)}, u32[]{:S(2)}) collective-permute-start(bf16[1040,128]{1,0:T(8,128)(2,1)S(1)} %collective-permute-done.37.buf_ref.rest_8_), channel_id=1, source_target_pairs={{0,1},{1,0},{2,3},{3,2},{4,5},{5,4},{6,7},{7,6},{8,9},{9,8},{10,11... | collective-permute-start | bytes 798728 | tf_op jit(solution)/shard_map/ppermute | solution.py:268
  88.1 6.9 %collective-permute-start.43 = (bf16[1040,128]{1,0:T(8,128)(2,1)S(1)}, bf16[1040,128]{1,0:T(8,128)(2,1)S(1)}, u32[]{:S(2)}, u32[]{:S(2)}) collective-permute-start(bf16[1040,128]{1,0:T(8,128)(2,1)S(1)} %collective-permute-done.39.buf_ref.rest_10_), channel_id=1, source_target_pairs={{0,4},{5,1},{4,8},{9,5},{8,12},{13,9},{12,14},{15,13},{14,10},{11,... | collective-permute-start | bytes 798728 | tf_op jit(solution)/shard_map/ppermute | solution.py:271
  90.4 3.7 %collective-permute-start.40 = (bf16[1040,128]{1,0:T(8,128)(2,1)S(1)}, bf16[1040,128]{1,0:T(8,128)(2,1)S(1)}, u32[]{:S(2)}, u32[]{:S(2)}) collective-permute-start(bf16[1040,128]{1,0:T(8,128)(2,1)S(1)} %collective-permute-done.39.buf_ref.rest_10_), channel_id=1, source_target_pairs={{0,1},{1,0},{2,3},{3,2},{4,5},{5,4},{6,7},{7,6},{8,9},{9,8},{10,11... | collective-permute-start | bytes 798728 | tf_op jit(solution)/shard_map/ppermute | solution.py:268
  91.7 4.0 %collective-permute-start.42 = (bf16[1040,128]{1,0:T(8,128)(2,1)S(1)}, bf16[1040,128]{1,0:T(8,128)(2,1)S(1)}, u32[]{:S(2)}, u32[]{:S(2)}) collective-permute-start(bf16[1040,128]{1,0:T(8,128)(2,1)S(1)} %collective-permute-done.41.buf_ref.rest_12_), channel_id=1, source_target_pairs={{0,1},{1,0},{2,3},{3,2},{4,5},{5,4},{6,7},{7,6},{8,9},{9,8},{10,11... | collective-permute-start | bytes 798728 | tf_op jit(solution)/shard_map/ppermute | solution.py:268
  95.0 1.6 %collective-permute-start.44 = (bf16[1040,128]{1,0:T(8,128)(2,1)S(1)}, bf16[1040,128]{1,0:T(8,128)(2,1)S(1)}, u32[]{:S(2)}, u32[]{:S(2)}) collective-permute-start(bf16[1040,128]{1,0:T(8,128)(2,1)S(1)} %collective-permute-done.43.buf_ref.rest_14_), channel_id=1, source_target_pairs={{0,1},{1,0},{2,3},{3,2},{4,5},{5,4},{6,7},{7,6},{8,9},{9,8},{10,11... | collective-permute-start | bytes 798728 | tf_op jit(solution)/shard_map/ppermute | solution.py:268
  99.6 4.6 %collective-permute-start.45 = (f32[8,128]{1,0:T(8,128)S(1)}, f32[8,128]{1,0:T(8,128)S(1)}, u32[]{:S(2)}, u32[]{:S(2)}) collective-permute-start(f32[8,128]{1,0:T(8,128)S(1)} %get-tuple-element.54), channel_id=1, source_target_pairs={{0,8},{1,9},{2,10},{3,11},{4,12},{5,13},{6,14},{7,15},{8,0},{9,1},... | collective-permute-start | bytes 12296 | tf_op jit(solution)/shard_map/ppermute | solution.py:413
  104.2 3.6 %collective-permute-start.46 = (f32[8,128]{1,0:T(8,128)S(1)}, f32[8,128]{1,0:T(8,128)S(1)}, u32[]{:S(2)}, u32[]{:S(2)}) collective-permute-start(f32[8,128]{1,0:T(8,128)S(1)} %add.16), channel_id=1, source_target_pairs={{0,4},{1,5},{2,6},{3,7},{4,0},{5,1},{6,2},{7,3},{8,12},{9,13},{10,... | collective-permute-start | bytes 12296 | tf_op jit(solution)/shard_map/ppermute | solution.py:413
  107.8 3.6 %collective-permute-start.47 = (f32[8,128]{1,0:T(8,128)S(1)}, f32[8,128]{1,0:T(8,128)S(1)}, u32[]{:S(2)}, u32[]{:S(2)}) collective-permute-start(f32[8,128]{1,0:T(8,128)S(1)} %add.17), channel_id=1, source_target_pairs={{0,2},{1,3},{2,0},{3,1},{4,6},{5,7},{6,4},{7,5},{8,10},{9,11},{10,... | collective-permute-start | bytes 12296 | tf_op jit(solution)/shard_map/ppermute | solution.py:413
  (6 other events, 27.2 us)
